TPU v7x, 512 devices: a whole 4x4x16 slice. The times are simulated.
512 devices in a mesh: row: 32 (over y, z_lo, core), col: 16 (over z_hi, x).
Axes of the slice: x: 4, y: 4, z: 16 (z_hi: 4, z_lo: 4; z = z_hi * 4 + z_lo), core: 2. Of those that a mesh axis runs over, the one named last changes fastest.
Arguments:
- activations: bfloat16 [1024, 14848], P('col', 'row'), may hold values from -6 to 6
- output_grads: bfloat16 [1024, 29696], P('row', 'col'), may hold values from -1 to 1
- weight: bfloat16 [14848, 29696], P('row', 'col'), may hold values from -0.046875 to 0.046875
- step_sizes: float32 [29696], P('col'), may hold values from 0.00012207031 to 0.001953125, as said below
- level_low: int32 [1], replicated, may hold values from -128 to -33
- level_high: int32 [1], replicated, may hold values from 32 to 127
Outputs:
- input_grads: bfloat16 [1024, 14848], P('col', 'row')
- weight_grads: bfloat16 [14848, 29696], P('row', 'col')
- step_grads: float32 [29696], P('col')
Inputs may be any that keep to these rules, and one draw needn't show every extreme that they name: `step_sizes`: every step size is one of the five powers of two 2^-13, 2^-12, 2^-11, 2^-10, 2^-9, each taken by about a fifth of the channels.
All inputs are finite; a program needn't handle non-finite values.
Results may differ from a plain program's by a relative error of at most 0.017.
Values may be sent and summed in bfloat16 or wider, within the bound.
No kernel may reach another device: no remote copies, remote signals or barrier semaphores. Data moves between devices by JAX's collectives and lax.ppermute only.
A program may use at most 64 MiB of HBM per device.

v0:
```python
import jax
import jax.numpy as jnp
from jax import lax
from jax.sharding import PartitionSpec as P


def quantize(weight, steps, low, high):
    ratio = weight.astype(jnp.float32) / steps[None, :]
    levels = jnp.clip(jnp.floor(ratio + 0.5), low, high)
    inside = jnp.logical_and(ratio >= low, ratio <= high)
    quantized = (levels * steps[None, :]).astype(jnp.bfloat16)
    coefficient = jnp.where(inside, levels - ratio, levels)
    return (quantized, inside.astype(jnp.float32), coefficient)


def shards(activations, output_grads, weight, step_sizes, level_low, level_high):
    low = level_low[0].astype(jnp.float32)
    high = level_high[0].astype(jnp.float32)
    quantized, inside, coefficient = quantize(weight, step_sizes, low, high)
    gathered = lax.all_gather(activations, "col", axis=0, tiled=True)
    contract_rows = (((0,), (0,)), ((), ()))
    contract_cols = (((1,), (1,)), ((), ()))
    grads = lax.all_gather(output_grads, "row", axis=0, tiled=True)
    wgrad = lax.dot_general(gathered, grads, contract_rows, preferred_element_type=jnp.float32)
    partial_rows = lax.dot_general(
        grads, quantized, contract_cols, preferred_element_type=jnp.float32
    )
    input_grads = lax.psum_scatter(
        partial_rows.astype(jnp.bfloat16), "col", scatter_dimension=0, tiled=True
    )
    weight_grads = (wgrad * inside).astype(jnp.bfloat16)
    local_sums = jnp.sum(wgrad * coefficient, axis=0)
    features = weight.shape[0] * lax.axis_size("row")
    scale = 1.0 / jnp.sqrt(jnp.float32(features) * high)
    step_grads = lax.psum(local_sums, "row") * scale
    return (input_grads, weight_grads, step_grads)


def solution(mesh):
    placed = (P("col", "row"), P("row", "col"), P("row", "col"), P("col"), P(), P())
    return jax.shard_map(
        shards,
        mesh=mesh,
        in_specs=placed,
        out_specs=(P("col", "row"), P("row", "col"), P("col")),
        check_vma=False,
    )
```

profile of v0, /device:TPU:1, one launch (start us, length us, event | category | flops | bytes accessed | tf_op | source)
XLA Modules:
  0.0 225.5 jit_solution(12088654004624778521)
XLA Ops:
  7.2 0.0 all-gather.2.cloned.1.call-start
  7.2 0.7 all-gather.2.cloned.1.call-update
  7.9 0.0 reduce-scatter.4.cloned.1.call-start
  9.3 77.0 %all_gather.7 = bf16[1024,464]{1,0:T(8,128)(2,1)S(1)} all-gather(bf16[64,464]{1,0:T(8,128)(2,1)} %param.6), channel_id=1, replica_groups=mesh['row'=32,'col'=16] {'col'}, dimensions={0}, use_global_device_ids=true | all-gather | bytes 1009664 | tf_op jit(solution)/shard_map/all_gather | solution.py:20
  86.3 10.1 %all-gather.2.cloned.1.call-done = bf16[1024,1856]{1,0:T(8,128)(2,1)} async-done(((bf16[32,1856]{1,0:T(8,128)(2,1)}), bf16[1024,1856]{1,0:T(8,128)(2,1)}) %all-gather.2.cloned.1.call-update) | async-done | bytes 3801104 | tf_op jit(solution)/shard_map/all_gather | solution.py:23
  96.4 0.0 copy-start
  96.4 0.0 copy-start.1
  96.4 5.9 %fusion.8 = bf16[1024,464]{0,1:T(8,128)(2,1)} fusion(bf16[1024,1856]{1,0:T(8,128)(2,1)} %all-gather.2.cloned.1.call-done, f32[1856]{0:T(1024)} %param.9, f32[]{:T(128)} %bitcast.1, f32[]{:T(128)} %bitcast, bf16[464,1856]{1,0:T(8,128)(2,1)} %param.8), kind=kOutput, calls=%fused_computation.14 | convolution fusion | flops 1771069440 | bytes 6481160 | tf_op jit(solution)/shard_map/dot_general | solution.py:25
  102.3 2.3 %copy.11 = bf16[1024,464]{1,0:T(8,128)(2,1)} copy(bf16[1024,464]{0,1:T(8,128)(2,1)} %fusion.8) | data formatting | bytes 1900544
  104.6 0.0 reduce-scatter.4.cloned.1.call-update
  104.6 0.0 copy-done
  104.6 0.0 copy-done.1
  104.6 6.0 %select_convert_fusion = (bf16[464,1856]{1,0:T(8,128)(2,1)}, f32[464,1856]{1,0:T(8,128)S(1)}) fusion(f32[]{:T(128)} %bitcast.1, f32[]{:T(128)} %bitcast, f32[1856]{0:T(1024)S(1)} %copy-done.1, bf16[464,1856]{1,0:T(8,128)(2,1)S(1)} %copy-done, bf16[1024,464]{1,0:T(8,128)(2,1)S(1)} %all_gather.7, bf16[1024,1856]{1,0:T(8,128)(2,1)} %all-gather.2.cloned.1.call-done), kind=kOutput, calls=%fused_computation.3 | convolution fusion | flops 1768871936 | bytes 11648264 | tf_op jit(solution)/shard_map/dot_general | solution.py:24
  110.6 1.5 fusion.1
  112.1 70.1 %psum.7 = f32[1856]{0:T(1024)S(1)} all-reduce(f32[1856]{0:T(1024)S(1)} %fusion.1), channel_id=1, replica_groups=mesh['row'=32,'col'=16] {'row'}, use_global_device_ids=true, to_apply=%region_2.3 | all-reduce | flops 1856 | bytes 14848 | tf_op jit(solution)/shard_map/psum | solution.py:35
  182.3 0.6 broadcast_multiply_fusion
  182.9 35.7 %reduce-scatter.4.cloned.1.call-done = bf16[64,464]{1,0:T(8,128)(2,1)} async-done(((bf16[1024,464]{1,0:T(8,128)(2,1)}), bf16[64,464]{1,0:T(8,128)(2,1)}) %reduce-scatter.4.cloned.1.call-update) | async-done | bytes 59408
Async XLA Ops:
  7.2 89.2 %all-gather.2.cloned.1.call-start = ((), (), s32[]{:S(2)}) async-start(), calls=%async_computation.1 | async-start | bytes 4055040 | tf_op jit(solution)/shard_map/all_gather | solution.py:23
  7.9 210.7 %reduce-scatter.4.cloned.1.call-start = ((), (), s32[]{:S(2)}) async-start(), calls=%async_computation.2 | async-start | bytes 1114112
  96.4 8.2 %copy-start = (bf16[464,1856]{1,0:T(8,128)(2,1)S(1)}, bf16[464,1856]{1,0:T(8,128)(2,1)}, u32[]{:S(2)}) copy-start(bf16[464,1856]{1,0:T(8,128)(2,1)} %param.8) | copy-start | bytes 5167108
  96.4 8.2 %copy-start.1 = (f32[1856]{0:T(1024)S(1)}, f32[1856]{0:T(1024)}, u32[]{:S(2)}) copy-start(f32[1856]{0:T(1024)} %param.9) | copy-start | bytes 22276
Sparse Core Ops, SparseCore 0:
  10.1 86.2 all-gather.1
  104.7 113.8 reduce-scatter.3
where the time goes:
time: 226 us; the launch traced here: 225 us
  blocking collectives  147 us (65%)
  waiting for transfers between devices  46.5 us (21%)
  between operations  15.4 us (7%)
  matrix products  11.9 us (5%)
  local copies, waits for them, and re-layouts  2.27 us (1%)
    all_gather x1, blocking collectives, shards(): gathered = lax.all_gather(activations, 'col', axis=0, tiled=True)  77 us
    psum x1, blocking collectives, shards(): step_grads = lax.psum(local_sums, 'row') * scale  70.1 us
    unnamed x3, waiting for transfers between devices  36.4 us
    all_gather x1, waiting for transfers between devices, shards(): grads = lax.all_gather(output_grads, 'row', axis=0, tiled=True)  10.1 us
    dot_general x1, matrix products, shards(): lax.dot_general(gathered, grads, contract_rows, preferred_element_type=jn...  5.98 us
    dot_general x1, matrix products, shards(): lax.dot_general(grads, quantized, contract_cols, preferred_element_type=j...  5.9 us
  transfers between devices with their start and end apart: 2, of which 2 were waited for; matrix products, arithmetic and copies ran while one was open for 4% of the time, Pallas kernels for 0%

commit v1 on v0

v1 whole, which is shorter than its diff:
```python
import jax
import jax.numpy as jnp
from jax import lax
from jax.sharding import Mesh, PartitionSpec as P

ROW = ("y", "zl", "c")
COL = ("zh", "x")


def quantize(weight, steps, low, high):
    ratio = weight.astype(jnp.float32) / steps[None, :]
    levels = jnp.clip(jnp.floor(ratio + 0.5), low, high)
    inside = jnp.logical_and(ratio >= low, ratio <= high)
    quantized = (levels * steps[None, :]).astype(jnp.bfloat16)
    coefficient = jnp.where(inside, levels - ratio, levels)
    return (quantized, inside.astype(jnp.float32), coefficient)


def shards(activations, output_grads, weight, step_sizes, level_low, level_high):
    f32, bf16 = jnp.float32, jnp.bfloat16
    low = level_low[0].astype(f32)
    high = level_high[0].astype(f32)
    quantized, inside, coefficient = quantize(weight, step_sizes, low, high)
    features, channels = weight.shape
    core = lax.axis_index("c")

    act = activations.reshape(2, 32, features)
    act = jnp.where(core == 0, act, act[::-1])
    act = lax.all_gather(act, "zh", axis=0)
    act = lax.all_gather(act, "x", axis=0)

    grads = lax.all_gather(output_grads, "zl", axis=0)
    pieces = []
    for p in range(2):
        own = lax.all_gather(grads[2 * p : 2 * p + 2], "y", axis=0)
        other = lax.ppermute(own, "c", [(0, 1), (1, 0)])
        pieces += [own, other]
    grads = jnp.stack(pieces).reshape(2, 2, 4, 2, 32, channels)
    rows = grads.reshape(1024, channels)
    act = act.reshape(2, 2, 4, 2, 32, features).transpose(0, 3, 2, 1, 4, 5).reshape(1024, features)

    partial_rows = lax.dot_general(
        rows, quantized, (((1,), (1,)), ((), ())), preferred_element_type=f32
    ).astype(bf16)
    sums = partial_rows.reshape(2, 2, 4, 2, 32, features).transpose(0, 3, 2, 1, 4, 5)
    sums = sums.reshape(4, 4, 64, features)
    sums = lax.all_to_all(sums, "x", 0, 0)
    sums = jnp.sum(sums.astype(f32), axis=0).astype(bf16)
    sums = lax.all_to_all(sums, "zh", 0, 0)
    sums = jnp.sum(sums.astype(f32), axis=0).astype(bf16).reshape(2, 32, features)
    input_grads = jnp.where(core == 0, sums, sums[::-1]).reshape(64, features)

    wgrad = lax.dot_general(act, rows, (((0,), (0,)), ((), ())), preferred_element_type=f32)
    weight_grads = (wgrad * inside).astype(bf16)
    local = jnp.sum(wgrad * coefficient, axis=0)
    scale = 1.0 / jnp.sqrt(f32(features * 32) * high)
    total = lax.psum(lax.psum(lax.psum(local, "c"), "zl"), "y")
    return (input_grads, weight_grads, total * scale)


def solution(mesh):
    fine = Mesh(mesh.devices.reshape(4, 4, 2, 4, 4), ROW + COL)
    placed = (P(COL, ROW), P(ROW, COL), P(ROW, COL), P(COL), P(), P())
    return jax.shard_map(
        shards,
        mesh=fine,
        in_specs=placed,
        out_specs=(P(COL, ROW), P(ROW, COL), P(COL)),
        check_vma=False,
    )
```

time: 226 us -> 158 us (0.70)
  the two profiles are of different devices: /device:TPU:1 before, /device:TPU:2 now
where the time goes in v1:
time: 158 us
  blocking collectives  114 us (72%)
  starting transfers between devices  16.1 us (10%)
  matrix products  10.5 us (7%)
  other arithmetic  7.58 us (5%)
  local copies, waits for them, and re-layouts  5.73 us (4%)
  between operations  2.11 us (1%)
  waiting for transfers between devices  2.06 us (1%)
    all_gather x2, blocking collectives, shards(): own = lax.all_gather(grads[2 * p:2 * p + 2], 'y', axis=0)  30.7 us
    all_gather x1, blocking collectives, shards(): act = lax.all_gather(act, 'zh', axis=0)  27.3 us
    psum x3, blocking collectives, shards(): total = lax.psum(lax.psum(lax.psum(local, 'c'), 'zl'), 'y')  24.7 us
    all_gather x1, blocking collectives, shards(): grads = lax.all_gather(output_grads, 'zl', axis=0)  16.9 us
    all_gather x1, blocking collectives, shards(): act = lax.all_gather(act, 'x', axis=0)  13.9 us
    dot_general x1, matrix products, shards(): lax.dot_general(act, rows, (((0,), (0,)), ((), ())), preferred_element_ty...  7.38 us
    all_to_all x1, starting transfers between devices, shards(): sums = lax.all_to_all(sums, 'zh', 0, 0)  6.55 us
    all_to_all x1, starting transfers between devices, shards(): sums = lax.all_to_all(sums, 'x', 0, 0)  5.71 us
  transfers between devices with their start and end apart: 4, of which 1 were waited for; matrix products, arithmetic and copies ran while one was open for 8% of the time, Pallas kernels for 0%

profile of v1, /device:TPU:2, one launch (start us, length us, event | category | flops | bytes accessed | tf_op | source)
XLA Modules:
  0.0 157.6 jit_solution(15661677290794421963)
XLA Ops:
  0.6 0.0 copy-start.3
  0.6 16.9 %all-gather = bf16[128,1856]{1,0:T(8,128)(2,1)S(1)} all-gather(bf16[32,1856]{1,0:T(8,128)(2,1)} %param.7), channel_id=2, replica_groups=mesh['y'=4,'zl'=4,'c'=2,'zh'=4,'x'=4] {'zl'}, dimensions={0}, use_global_device_ids=true | all-gather | bytes 593920 | tf_op jit(solution)/shard_map/all_gather | solution.py:32
  17.6 15.5 %all-gather.1 = bf16[8,32,1856]{2,1,0:T(8,128)(2,1)S(1)} all-gather(bf16[2,32,1856]{2,1,0:T(8,128)(2,1)S(1)} %bitcast.37), channel_id=3, replica_groups=mesh['y'=4,'zl'=4,'c'=2,'zh'=4,'x'=4] {'y'}, dimensions={0}, use_global_device_ids=true | all-gather | bytes 1187840 | tf_op jit(solution)/shard_map/all_gather | solution.py:35
  33.1 1.9 %collective-permute-start = (bf16[4,2,32,1856]{3,2,1,0:T(8,128)(2,1)S(1)}, bf16[4,2,32,1856]{3,2,1,0:T(8,128)(2,1)S(1)}, u32[]{:S(2)}, u32[]{:S(2)}) collective-permute-start(bf16[4,2,32,1856]{3,2,1,0:T(8,128)(2,1)S(1)} %bitcast.30), channel_id=1, source_target_pairs={{0,16},{16,0},{1,17},{17,1},{2,18},{18,2},{3,19},{19,3},{4,20},{20... | collective-permute-start | bytes 2850824 | tf_op jit(solution)/shard_map/ppermute | solution.py:36
  35.0 15.2 %all-gather.2 = bf16[8,32,1856]{2,1,0:T(8,128)(2,1)S(1)} all-gather(bf16[2,32,1856]{2,1,0:T(8,128)(2,1)S(1)} %bitcast.36), channel_id=4, replica_groups=mesh['y'=4,'zl'=4,'c'=2,'zh'=4,'x'=4] {'y'}, dimensions={0}, use_global_device_ids=true | all-gather | bytes 1187840 | tf_op jit(solution)/shard_map/all_gather | solution.py:35
  50.2 1.9 %collective-permute-start.1 = (bf16[4,2,32,1856]{3,2,1,0:T(8,128)(2,1)S(1)}, bf16[4,2,32,1856]{3,2,1,0:T(8,128)(2,1)}, u32[]{:S(2)}, u32[]{:S(2)}) collective-permute-start(bf16[4,2,32,1856]{3,2,1,0:T(8,128)(2,1)S(1)} %bitcast.32), channel_id=1, source_target_pairs={{0,16},{16,0},{1,17},{17,1},{2,18},{18,2},{3,19},{19,3},{4,20},{20... | collective-permute-start | bytes 2850824 | tf_op jit(solution)/shard_map/ppermute | solution.py:36
  53.5 0.0 copy-done.3
  53.5 27.3 %all-gather.3 = bf16[8,32,464]{2,1,0:T(8,128)(2,1)S(1)} all-gather(bf16[2,32,464]{2,1,0:T(8,128)(2,1)S(1)} %reverse_select_fusion), channel_id=5, replica_groups=mesh['y'=4,'zl'=4,'c'=2,'zh'=4,'x'=4] {'zh'}, dimensions={0}, use_global_device_ids=true | all-gather | bytes 296960 | tf_op jit(solution)/shard_map/all_gather | solution.py:29
  80.7 13.9 %all-gather.4 = bf16[16,2,32,464]{3,2,1,0:T(8,128)(2,1)S(1)} all-gather(bf16[4,2,32,464]{3,2,1,0:T(8,128)(2,1)S(1)} %bitcast.34), channel_id=6, replica_groups=mesh['y'=4,'zl'=4,'c'=2,'zh'=4,'x'=4] {'x'}, dimensions={0}, use_global_device_ids=true | all-gather | bytes 1187840 | tf_op jit(solution)/shard_map/all_gather | solution.py:30
  94.6 1.1 copy.19
  95.8 0.0 collective-permute-done
  95.8 0.0 collective-permute-done.1
  95.8 0.0 copy-start.1
  95.8 0.0 copy-start.4
  95.8 1.8 %pad_maximum_fusion = bf16[4,4,2,32,1856]{4,3,2,1,0:T(8,128)(2,1)S(1)} fusion(bf16[1,4,2,32,1856]{4,3,2,1,0:T(8,128)(2,1)} %bitcast.7, bf16[1,4,2,32,1856]{4,3,2,1,0:T(8,128)(2,1)S(1)} %bitcast.33, bf16[1,4,2,32,1856]{4,3,2,1,0:T(8,128)(2,1)S(1)} %bitcast.38, bf16[1,4,2,32,1856]{4,3,2,1,0:T(8,128)(2,1)S(1)} %bitcast.31), kind=kLoop, calls=%fused_computation.1 | loop fusion | flops 5701632 | bytes 7602176 | tf_op jit(solution)/shard_map/stack | solution.py:38
  97.6 0.0 copy-start
  97.6 1.9 %copy-done = bf16[4,4,2,32,1856]{4,3,2,1,0:T(8,128)(2,1)} copy-done((bf16[4,4,2,32,1856]{4,3,2,1,0:T(8,128)(2,1)}, bf16[4,4,2,32,1856]{4,3,2,1,0:T(8,128)(2,1)S(1)}, u32[]{:S(2)}) %copy-start) | copy-done | bytes 3801112
  99.5 0.0 copy-done.1
  99.5 0.0 copy-done.4
  99.5 3.1 %fusion.7 = bf16[1024,464]{0,1:T(8,128)(2,1)} fusion(bf16[1024,1856]{1,0:T(8,128)(2,1)S(1)} %bitcast.28, f32[1856]{0:T(1024)S(1)} %copy-done.4, f32[]{:T(128)} %bitcast.10, f32[]{:T(128)} %bitcast.9, bf16[464,1856]{1,0:T(8,128)(2,1)S(1)} %copy-done.1), kind=kOutput, calls=%fused_computation.14 | convolution fusion | flops 1771069440 | bytes 6481160 | tf_op jit(solution)/shard_map/dot_general | solution.py:42
  102.6 0.0 copy-start.2
  102.6 1.6 %copy.17 = bf16[1024,464]{1,0:T(8,128)(2,1)S(1)} copy(bf16[1024,464]{0,1:T(8,128)(2,1)} %fusion.7) | data formatting | bytes 1900544 | tf_op jit(solution)/shard_map/convert_element_type | solution.py:44
  104.2 1.1 copy.18
  105.4 5.7 %all-to-all-start = ((bf16[4,4,64,464]{3,2,1,0:T(8,128)(2,1)}), bf16[4,4,64,464]{3,2,1,0:T(8,128)(2,1)S(1)}, u32[]{:S(2)}, u32[]{:S(2)}) async-start(bf16[4,4,64,464]{3,2,1,0:T(8,128)(2,1)} %bitcast.13), calls=%async_computation | async-start | bytes 2097152 | tf_op jit(solution)/shard_map/all_to_all | solution.py:47
  111.1 0.0 copy-done.2
  111.1 7.4 %select_convert_fusion = (bf16[464,1856]{1,0:T(8,128)(2,1)}, f32[464,1856]{1,0:T(8,128)}) fusion(f32[]{:T(128)} %bitcast.10, f32[]{:T(128)} %bitcast.9, f32[1856]{0:T(1024)S(1)} %copy-done.4, bf16[464,1856]{1,0:T(8,128)(2,1)S(1)} %copy-done.2, bf16[1024,464]{1,0:T(8,128)(2,1)} %bitcast.35, bf16[1024,1856]{1,0:T(8,128)(2,1)} %bitcast.29), kind=kOutput, calls=%fused_computation.4 | convolution fusion | flops 1768871936 | bytes 11648264 | tf_op jit(solution)/shard_map/dot_general | solution.py:53
  118.5 2.1 %all-to-all-done = bf16[4,4,64,464]{3,2,1,0:T(8,128)(2,1)S(1)} async-done(((bf16[4,4,64,464]{3,2,1,0:T(8,128)(2,1)}), bf16[4,4,64,464]{3,2,1,0:T(8,128)(2,1)S(1)}, u32[]{:S(2)}, u32[]{:S(2)}) %all-to-all-start) | async-done | bytes 950304 | tf_op jit(solution)/shard_map/all_to_all | solution.py:47
  120.5 0.9 reduce_sum.33
  121.4 6.5 %all-to-all-start.1 = ((bf16[4,64,464]{2,1,0:T(8,128)(2,1)}), bf16[4,64,464]{2,1,0:T(8,128)(2,1)S(1)}, u32[]{:S(2)}, u32[]{:S(2)}) async-start(bf16[4,64,464]{2,1,0:T(8,128)(2,1)} %reduce_sum.33), calls=%async_computation.1 | async-start | bytes 524288 | tf_op jit(solution)/shard_map/all_to_all | solution.py:49
  128.0 3.5 %fusion.1 = f32[1856]{0:T(1024)S(1)} fusion(f32[464,1856]{1,0:T(8,128)} %get-tuple-element.6, f32[]{:T(128)} %bitcast.10, f32[]{:T(128)} %bitcast.9, f32[1856]{0:T(1024)S(1)} %copy-done.4, bf16[464,1856]{1,0:T(8,128)(2,1)S(1)} %copy-done.2), kind=kLoop, calls=%fused_computation.3 | loop fusion | flops 11193536 | bytes 5181960 | tf_op jit(solution)/shard_map/reduce_sum | solution.py:55
  131.5 2.5 %psum.21 = f32[1856]{0:T(1024)S(1)} all-reduce(f32[1856]{0:T(1024)S(1)} %fusion.1), channel_id=1, replica_groups=mesh['y'=4,'zl'=4,'c'=2,'zh'=4,'x'=4] {'c'}, use_global_device_ids=true, to_apply=%region_3.4 | all-reduce | flops 1856 | bytes 14848 | tf_op jit(solution)/shard_map/psum | solution.py:57
  134.0 13.0 %psum.22 = f32[1856]{0:T(1024)S(1)} all-reduce(f32[1856]{0:T(1024)S(1)} %psum.21), channel_id=1, replica_groups=mesh['y'=4,'zl'=4,'c'=2,'zh'=4,'x'=4] {'zl'}, use_global_device_ids=true, to_apply=%region_4.5 | all-reduce | flops 1856 | bytes 14848 | tf_op jit(solution)/shard_map/psum | solution.py:57
  147.0 9.3 %psum.23 = f32[1856]{0:T(1024)S(1)} all-reduce(f32[1856]{0:T(1024)S(1)} %psum.22), channel_id=1, replica_groups=mesh['y'=4,'zl'=4,'c'=2,'zh'=4,'x'=4] {'y'}, use_global_device_ids=true, to_apply=%region_5.6 | all-reduce | flops 1856 | bytes 14848 | tf_op jit(solution)/shard_map/psum | solution.py:57
  156.3 0.6 broadcast_multiply_fusion
  156.9 0.0 all-to-all-done.1
  156.9 0.6 reverse_select_fusion.1
  (3 shorter events, 0.1 us)
Async XLA Ops:
  0.6 52.8 %copy-start.3 = (bf16[64,464]{1,0:T(8,128)(2,1)S(1)}, bf16[64,464]{1,0:T(8,128)(2,1)}, u32[]{:S(2)}) copy-start(bf16[64,464]{1,0:T(8,128)(2,1)} %param.6) | copy-start | bytes 178180
  33.1 62.7 %collective-permute-start = (bf16[4,2,32,1856]{3,2,1,0:T(8,128)(2,1)S(1)}, bf16[4,2,32,1856]{3,2,1,0:T(8,128)(2,1)S(1)}, u32[]{:S(2)}, u32[]{:S(2)}) collective-permute-start(bf16[4,2,32,1856]{3,2,1,0:T(8,128)(2,1)S(1)} %bitcast.30), channel_id=1, source_target_pairs={{0,16},{16,0},{1,17},{17,1},{2,18},{18,2},{3,19},{19,3},{4,20},{20... | collective-permute-start | bytes 2850824 | tf_op jit(solution)/shard_map/ppermute | solution.py:36
  50.2 45.5 %collective-permute-start.1 = (bf16[4,2,32,1856]{3,2,1,0:T(8,128)(2,1)S(1)}, bf16[4,2,32,1856]{3,2,1,0:T(8,128)(2,1)}, u32[]{:S(2)}, u32[]{:S(2)}) collective-permute-start(bf16[4,2,32,1856]{3,2,1,0:T(8,128)(2,1)S(1)} %bitcast.32), channel_id=1, source_target_pairs={{0,16},{16,0},{1,17},{17,1},{2,18},{18,2},{3,19},{19,3},{4,20},{20... | collective-permute-start | bytes 2850824 | tf_op jit(solution)/shard_map/ppermute | solution.py:36
  95.8 3.7 %copy-start.1 = (bf16[464,1856]{1,0:T(8,128)(2,1)S(1)}, bf16[464,1856]{1,0:T(8,128)(2,1)}, u32[]{:S(2)}) copy-start(bf16[464,1856]{1,0:T(8,128)(2,1)} %param.8) | copy-start | bytes 5167108
  95.8 3.7 %copy-start.4 = (f32[1856]{0:T(1024)S(1)}, f32[1856]{0:T(1024)}, u32[]{:S(2)}) copy-start(f32[1856]{0:T(1024)} %param.9) | copy-start | bytes 22276
  97.6 1.9 %copy-start = (bf16[4,4,2,32,1856]{4,3,2,1,0:T(8,128)(2,1)}, bf16[4,4,2,32,1856]{4,3,2,1,0:T(8,128)(2,1)S(1)}, u32[]{:S(2)}) copy-start(bf16[4,4,2,32,1856]{4,3,2,1,0:T(8,128)(2,1)S(1)} %pad_maximum_fusion) | copy-start | bytes 11403268
  102.6 8.4 %copy-start.2 = (bf16[464,1856]{1,0:T(8,128)(2,1)S(1)}, bf16[464,1856]{1,0:T(8,128)(2,1)}, u32[]{:S(2)}) copy-start(bf16[464,1856]{1,0:T(8,128)(2,1)} %param.8) | copy-start | bytes 5167108
  105.4 15.2 %all-to-all-start = ((bf16[4,4,64,464]{3,2,1,0:T(8,128)(2,1)}), bf16[4,4,64,464]{3,2,1,0:T(8,128)(2,1)S(1)}, u32[]{:S(2)}, u32[]{:S(2)}) async-start(bf16[4,4,64,464]{3,2,1,0:T(8,128)(2,1)} %bitcast.13), calls=%async_computation | async-start | bytes 2097152 | tf_op jit(solution)/shard_map/all_to_all | solution.py:47
  121.4 35.4 %all-to-all-start.1 = ((bf16[4,64,464]{2,1,0:T(8,128)(2,1)}), bf16[4,64,464]{2,1,0:T(8,128)(2,1)S(1)}, u32[]{:S(2)}, u32[]{:S(2)}) async-start(bf16[4,64,464]{2,1,0:T(8,128)(2,1)} %reduce_sum.33), calls=%async_computation.1 | async-start | bytes 524288 | tf_op jit(solution)/shard_map/all_to_all | solution.py:49

commit v2 on v1

v2 whole, which is shorter than its diff:
```python
import jax
import jax.numpy as jnp
from jax import lax
from jax.sharding import Mesh, PartitionSpec as P

ROW = ("y", "zl", "c")
COL = ("zh", "x")
SWAP = [(0, 1), (1, 0)]


def quantize(weight, steps, low, high):
    ratio = weight.astype(jnp.float32) / steps[None, :]
    levels = jnp.clip(jnp.floor(ratio + 0.5), low, high)
    inside = jnp.logical_and(ratio >= low, ratio <= high)
    quantized = (levels * steps[None, :]).astype(jnp.bfloat16)
    coefficient = jnp.where(inside, levels - ratio, levels)
    return (quantized, inside.astype(jnp.float32), coefficient)


def gather(block, axis):
    return lax.all_to_all(jnp.broadcast_to(block[None], (4, *block.shape)), axis, 0, 0)


def shards(activations, output_grads, weight, step_sizes, level_low, level_high):
    f32, bf16 = jnp.float32, jnp.bfloat16
    low = level_low[0].astype(f32)
    high = level_high[0].astype(f32)
    quantized, inside, coefficient = quantize(weight, step_sizes, low, high)
    features, channels = weight.shape
    core = lax.axis_index("c")

    grads = lax.all_gather(output_grads, "zl", axis=0)
    activations, grads = lax.optimization_barrier((activations, grads))
    grads = grads.reshape(4, 2, 16, channels)
    own = [gather(grads[:, h], "y") for h in range(2)]

    act = activations.reshape(2, 32, features)
    act = jnp.where(core == 0, act, act[::-1])
    act = gather(gather(act, "zh"), "x")
    act = act.reshape(4, 4, 2, 2, 16, features).transpose(3, 2, 1, 0, 4, 5)
    act = act.reshape(1024, features)

    rows, sums = [], []
    for h in range(2):
        both = jnp.concatenate([own[h], lax.ppermute(own[h], "c", SWAP)]).reshape(512, channels)
        rows.append(both)
        part = lax.dot_general(
            both, quantized, (((1,), (1,)), ((), ())), preferred_element_type=f32
        ).astype(bf16)
        part = part.reshape(2, 4, 4, 16, features).transpose(2, 1, 0, 3, 4)
        part = lax.all_to_all(part, "x", 0, 0)
        sums.append(jnp.sum(part.astype(f32), axis=0).astype(bf16))
    sums = lax.all_to_all(jnp.stack(sums, axis=2), "zh", 0, 0)
    sums = jnp.sum(sums.astype(f32), axis=0).astype(bf16).reshape(2, 32, features)
    input_grads = jnp.where(core == 0, sums, sums[::-1]).reshape(64, features)

    wgrad = lax.dot_general(
        act, jnp.concatenate(rows), (((0,), (0,)), ((), ())), preferred_element_type=f32
    )
    weight_grads = (wgrad * inside).astype(bf16)
    local = jnp.sum(wgrad * coefficient, axis=0)
    scale = 1.0 / jnp.sqrt(f32(features * 32) * high)
    total = lax.psum(lax.psum(lax.psum(local, "c"), "y"), "zl")
    return (input_grads, weight_grads, total * scale)


def solution(mesh):
    fine = Mesh(mesh.devices.reshape(4, 4, 2, 4, 4), ROW + COL)
    placed = (P(COL, ROW), P(ROW, COL), P(ROW, COL), P(COL), P(), P())
    return jax.shard_map(
        shards,
        mesh=fine,
        in_specs=placed,
        out_specs=(P(COL, ROW), P(ROW, COL), P(COL)),
        check_vma=False,
    )
```

time: 158 us -> 158 us (level)
  blocking collectives: 114 us -> 55.2 us
  waiting for transfers between devices: 2.06 us -> 30.2 us
  starting transfers between devices: 16.1 us -> 38.8 us
  local copies, waits for them, and re-layouts: 5.73 us -> 10.5 us
  matrix products: 10.5 us -> 12.1 us
    all_gather x4 -> x0, blocking collectives: 71.9 us -> none  [the longest x2 30.7 us: shards(): own = lax.all_gather(grads[2 * p:2 * p + 2], 'y', axis=0)]
    all_to_all x2 -> x6, waiting for transfers between devices: 2.06 us -> 30.2 us  [the longest x3 30.2 us: gather(): lax.all_to_all(jnp.broadcast_to(block[None], (4, *block.shape)), axis, 0, 0)]
    all_to_all x2 -> x6, starting transfers between devices: 12.3 us -> 34.9 us  [the longest x3 20.5 us: gather(): lax.all_to_all(jnp.broadcast_to(block[None], (4, *block.shape)), axis, 0, 0)]
    all_to_all x0 -> x1, blocking collectives: none -> 16.7 us  [gather(): lax.all_to_all(jnp.broadcast_to(block[None], (4, *block.shape)), axis, 0, 0)]
    psum x3, blocking collectives: 24.7 us -> 21.7 us  [shards(): total = lax.psum(lax.psum(lax.psum(local, 'c'), 'y'), 'zl')]
    broadcast_in_dim x0 -> x5, local copies, waits for them, and re-layouts: none -> 2.93 us  [gather(): jnp.broadcast_to(block[None], (4, *block.shape))]
    concatenate x0 -> x2, other arithmetic: none -> 2.82 us  [shards(): jnp.concatenate([own[h], lax.ppermute(own[h], 'c', SWAP)])]
    another operation x1, other arithmetic: 1.82 us -> 0.03 us  [shards(): sums = lax.all_to_all(jnp.stack(sums, axis=2), 'zh', 0, 0)]
  transfers between devices with their start and end apart: 4 -> 8, of which waited for: 1 -> 3; matrix products, arithmetic and copies ran while one was open for 8% -> 16% of each run, Pallas kernels for 0% -> 0%
where the time goes in v2:
time: 158 us; the launch traced here: 157 us
  blocking collectives  55.2 us (35%)
  starting transfers between devices  38.8 us (25%)
  waiting for transfers between devices  30.2 us (19%)
  matrix products  12.1 us (8%)
  local copies, waits for them, and re-layouts  10.5 us (7%)
  other arithmetic  7.87 us (5%)
  between operations  2.14 us (1%)
    all_to_all x3, waiting for transfers between devices, gather(): lax.all_to_all(jnp.broadcast_to(block[None], (4, *block.shape)), axis, 0, 0)  30.2 us
    psum x3, blocking collectives, shards(): total = lax.psum(lax.psum(lax.psum(local, 'c'), 'y'), 'zl')  21.7 us
    all_to_all x3, starting transfers between devices, gather(): lax.all_to_all(jnp.broadcast_to(block[None], (4, *block.shape)), axis, 0, 0)  20.5 us
    all_gather x1, blocking collectives, shards(): grads = lax.all_gather(output_grads, 'zl', axis=0)  16.8 us
    all_to_all x1, blocking collectives, gather(): lax.all_to_all(jnp.broadcast_to(block[None], (4, *block.shape)), axis, 0, 0)  16.7 us
    all_to_all x2, starting transfers between devices, shards(): part = lax.all_to_all(part, 'x', 0, 0)  9.7 us
    dot_general x1, matrix products, shards(): lax.dot_general(act, jnp.concatenate(rows), (((0,), (0,)), ((), ())), pre...  7.32 us
    dot_general x2, matrix products, shards(): lax.dot_general(both, quantized, (((1,), (1,)), ((), ())), preferred_elem...  4.82 us
  transfers between devices with their start and end apart: 8, of which 3 were waited for; matrix products, arithmetic and copies ran while one was open for 16% of the time, Pallas kernels for 0%

profile of v2, /device:TPU:2, one launch (start us, length us, event | category | flops | bytes accessed | tf_op | source)
XLA Modules:
  0.0 156.8 jit_solution(366082088626271885)
XLA Ops:
  0.6 16.8 %all-gather = bf16[128,1856]{1,0:T(8,128)(2,1)S(1)} all-gather(bf16[32,1856]{1,0:T(8,128)(2,1)} %param.7), channel_id=2, replica_groups=mesh['y'=4,'zl'=4,'c'=2,'zh'=4,'x'=4] {'zl'}, dimensions={0}, use_global_device_ids=true | all-gather | bytes 593920 | tf_op jit(solution)/shard_map/all_gather | solution.py:32
  17.4 0.1 broadcast_in_dim.13
  17.5 16.7 %all_to_all.35 = bf16[4,4,16,1856]{3,2,1,0:T(8,128)(2,1)S(1)} all-to-all(bf16[4,4,16,1856]{3,2,1,0:T(8,128)(2,1)S(1)} %broadcast_in_dim.13), channel_id=1, replica_groups=mesh['y'=4,'zl'=4,'c'=2,'zh'=4,'x'=4] {'y'}, dimensions={0} | all-to-all | bytes 1900544 | tf_op jit(solution)/shard_map/all_to_all | solution.py:21
  34.3 1.0 broadcast_in_dim.15
  35.3 3.5 %all-to-all-start.2 = ((bf16[4,4,16,1856]{3,2,1,0:T(8,128)(2,1)}), bf16[4,4,16,1856]{3,2,1,0:T(8,128)(2,1)S(1)}, u32[]{:S(2)}, u32[]{:S(2)}) async-start(bf16[4,4,16,1856]{3,2,1,0:T(8,128)(2,1)} %broadcast_in_dim.15), calls=%async_computation.2 | async-start | bytes 1966080 | tf_op jit(solution)/shard_map/all_to_all | solution.py:21
  38.8 0.0 copy-done.5
  38.8 11.5 %all-to-all-done.2 = bf16[4,4,16,1856]{3,2,1,0:T(8,128)(2,1)S(1)} async-done(((bf16[4,4,16,1856]{3,2,1,0:T(8,128)(2,1)}), bf16[4,4,16,1856]{3,2,1,0:T(8,128)(2,1)S(1)}, u32[]{:S(2)}, u32[]{:S(2)}) %all-to-all-start.2) | async-done | bytes 950304 | tf_op jit(solution)/shard_map/all_to_all | solution.py:21
  50.3 0.7 broadcast_in_dim.32
  51.0 12.0 %all-to-all-start.5 = ((bf16[4,2,32,464]{3,2,1,0:T(8,128)(2,1)}), bf16[4,2,32,464]{3,2,1,0:T(8,128)(2,1)S(1)}, u32[]{:S(2)}, u32[]{:S(2)}) async-start(bf16[4,2,32,464]{3,2,1,0:T(8,128)(2,1)} %broadcast_in_dim.32), calls=%async_computation.5 | async-start | bytes 524288 | tf_op jit(solution)/shard_map/all_to_all | solution.py:21
  63.0 1.9 %collective-permute-start = (bf16[4,4,16,1856]{3,2,1,0:T(8,128)(2,1)S(1)}, bf16[4,4,16,1856]{3,2,1,0:T(8,128)(2,1)}, u32[]{:S(2)}, u32[]{:S(2)}) collective-permute-start(bf16[4,4,16,1856]{3,2,1,0:T(8,128)(2,1)S(1)} %all_to_all.35), channel_id=1, source_target_pairs={{0,16},{16,0},{1,17},{17,1},{2,18},{18,2},{3,19},{19,3},{4,20},{20... | collective-permute-start | bytes 2850824 | tf_op jit(solution)/shard_map/ppermute | solution.py:45
  64.9 12.6 %all-to-all-done.5 = bf16[4,2,32,464]{3,2,1,0:T(8,128)(2,1)S(1)} async-done(((bf16[4,2,32,464]{3,2,1,0:T(8,128)(2,1)}), bf16[4,2,32,464]{3,2,1,0:T(8,128)(2,1)S(1)}, u32[]{:S(2)}, u32[]{:S(2)}) %all-to-all-start.5) | async-done | bytes 237600 | tf_op jit(solution)/shard_map/all_to_all | solution.py:21
  77.5 1.1 broadcast_in_dim.33
  78.6 5.0 %all-to-all-start.6 = ((bf16[4,4,2,32,464]{4,3,2,1,0:T(8,128)(2,1)}), bf16[4,4,2,32,464]{4,3,2,1,0:T(8,128)(2,1)S(1)}, u32[]{:S(2)}, u32[]{:S(2)}) async-start(bf16[4,4,2,32,464]{4,3,2,1,0:T(8,128)(2,1)} %broadcast_in_dim.33), calls=%async_computation.6 | async-start | bytes 2097152 | tf_op jit(solution)/shard_map/all_to_all | solution.py:21
  84.9 1.9 %collective-permute-start.1 = (bf16[4,4,16,1856]{3,2,1,0:T(8,128)(2,1)S(1)}, bf16[4,4,16,1856]{3,2,1,0:T(8,128)(2,1)}, u32[]{:S(2)}, u32[]{:S(2)}) collective-permute-start(bf16[4,4,16,1856]{3,2,1,0:T(8,128)(2,1)S(1)} %all-to-all-done.2), channel_id=1, source_target_pairs={{0,16},{16,0},{1,17},{17,1},{2,18},{18,2},{3,19},{19,3},{4,20},{20... | collective-permute-start | bytes 2850824 | tf_op jit(solution)/shard_map/ppermute | solution.py:45
  86.8 6.2 %all-to-all-done.6 = bf16[4,4,2,32,464]{4,3,2,1,0:T(8,128)(2,1)S(1)} async-done(((bf16[4,4,2,32,464]{4,3,2,1,0:T(8,128)(2,1)}), bf16[4,4,2,32,464]{4,3,2,1,0:T(8,128)(2,1)S(1)}, u32[]{:S(2)}, u32[]{:S(2)}) %all-to-all-start.6) | async-done | bytes 950304 | tf_op jit(solution)/shard_map/all_to_all | solution.py:21
  93.0 1.1 copy.38
  94.1 0.0 collective-permute-done
  94.1 1.4 pad_maximum_fusion
  95.5 0.0 copy-start
  95.5 1.3 copy-done
  96.8 0.0 copy-done.6
  96.8 1.2 convolution_convert_fusion.1
  98.0 0.2 copy.30
  98.3 0.8 copy.31
  99.1 4.9 %all-to-all-start.1 = ((bf16[4,4,2,16,464]{4,3,1,2,0:T(8,128)(2,1)}), bf16[4,4,2,16,464]{4,3,1,2,0:T(8,128)(2,1)S(1)}, u32[]{:S(2)}, u32[]{:S(2)}) async-start(bf16[4,4,2,16,464]{4,3,1,2,0:T(8,128)(2,1)} %copy.31), calls=%async_computation.1 | async-start | bytes 1048576 | tf_op jit(solution)/shard_map/all_to_all | solution.py:51
  104.0 0.0 collective-permute-done.1
  104.0 1.4 pad_maximum_fusion.1
  105.4 0.0 copy-start.2
  105.4 1.3 copy-done.2
  106.7 3.6 %convolution_convert_fusion = bf16[512,464]{0,1:T(8,128)(2,1)} fusion(bf16[512,1856]{1,0:T(8,128)(2,1)S(1)} %bitcast.33, f32[1856]{0:T(1024)S(1)} %copy-done.6, f32[]{:T(128)} %bitcast.5, f32[]{:T(128)} %bitcast.4, bf16[464,1856]{1,0:T(8,128)(2,1)} %param.8), kind=kOutput, calls=%fused_computation.14 | convolution fusion | flops 888979456 | bytes 4105480 | tf_op jit(solution)/shard_map/dot_general | solution.py:47
  110.3 1.2 copy.33
  111.6 0.8 copy.34
  112.4 0.0 all-to-all-done.1
  112.4 4.8 %all-to-all-start.3 = ((bf16[4,4,2,16,464]{4,3,1,2,0:T(8,128)(2,1)}), bf16[4,4,2,16,464]{4,3,1,2,0:T(8,128)(2,1)S(1)}, u32[]{:S(2)}, u32[]{:S(2)}) async-start(bf16[4,4,2,16,464]{4,3,1,2,0:T(8,128)(2,1)} %copy.34), calls=%async_computation.3 | async-start | bytes 1048576 | tf_op jit(solution)/shard_map/all_to_all | solution.py:51
  117.2 7.3 %select_convert_fusion = (bf16[464,1856]{1,0:T(8,128)(2,1)}, f32[464,1856]{1,0:T(8,128)}) fusion(f32[]{:T(128)} %bitcast.5, f32[]{:T(128)} %bitcast.4, f32[1856]{0:T(1024)S(1)} %copy-done.6, bf16[464,1856]{1,0:T(8,128)(2,1)} %param.8, bf16[1024,464]{1,0:T(8,128)(2,1)} %bitcast.36, bf16[512,1856]{1,0:T(8,128)(2,1)} %bitcast.34, bf16[512,1856]{1,0:T(8,128)(2,1)S(1)} %bitcast.32), kind=kOutput, calls=%fused_computation.7 | convolution fusion | flops 1776474112 | bytes 11648264 | tf_op jit(solution)/shard_map/dot_general | solution.py:57
  124.5 0.1 reduce_sum.45
  124.6 0.0 all-to-all-done.3
  124.6 0.1 reduce_sum.46
  124.8 0.7 copy.36
  125.5 4.8 %all-to-all-start.4 = ((bf16[4,2,2,16,464]{4,3,1,2,0:T(8,128)(2,1)}), bf16[4,2,2,16,464]{4,3,1,2,0:T(8,128)(2,1)S(1)}, u32[]{:S(2)}, u32[]{:S(2)}) async-start(bf16[4,2,2,16,464]{4,3,1,2,0:T(8,128)(2,1)} %copy.36), calls=%async_computation.4 | async-start | bytes 524288 | tf_op jit(solution)/shard_map/all_to_all | solution.py:53
  130.3 0.0 copy-done.4
  130.3 3.5 %fusion.5 = f32[1856]{0:T(1024)S(1)} fusion(f32[464,1856]{1,0:T(8,128)} %get-tuple-element.10, f32[]{:T(128)} %bitcast.5, f32[]{:T(128)} %bitcast.4, f32[1856]{0:T(1024)S(1)} %copy-done.6, bf16[464,1856]{1,0:T(8,128)(2,1)S(1)} %copy-done.4), kind=kLoop, calls=%fused_computation.6 | loop fusion | flops 11193536 | bytes 5181960 | tf_op jit(solution)/shard_map/reduce_sum | solution.py:61
  133.8 2.5 %psum.21 = f32[1856]{0:T(1024)S(1)} all-reduce(f32[1856]{0:T(1024)S(1)} %fusion.5), channel_id=1, replica_groups=mesh['y'=4,'zl'=4,'c'=2,'zh'=4,'x'=4] {'c'}, use_global_device_ids=true, to_apply=%region_4.5 | all-reduce | flops 1856 | bytes 14848 | tf_op jit(solution)/shard_map/psum | solution.py:63
  136.3 9.0 %psum.22 = f32[1856]{0:T(1024)S(1)} all-reduce(f32[1856]{0:T(1024)S(1)} %psum.21), channel_id=1, replica_groups=mesh['y'=4,'zl'=4,'c'=2,'zh'=4,'x'=4] {'y'}, use_global_device_ids=true, to_apply=%region_5.6 | all-reduce | flops 1856 | bytes 14848 | tf_op jit(solution)/shard_map/psum | solution.py:63
  145.3 10.2 %psum.23 = f32[1856]{0:T(1024)S(1)} all-reduce(f32[1856]{0:T(1024)S(1)} %psum.22), channel_id=1, replica_groups=mesh['y'=4,'zl'=4,'c'=2,'zh'=4,'x'=4] {'zl'}, use_global_device_ids=true, to_apply=%region_6.7 | all-reduce | flops 1856 | bytes 14848 | tf_op jit(solution)/shard_map/psum | solution.py:63
  155.5 0.6 broadcast_multiply_fusion
  156.1 0.0 all-to-all-done.4
  156.2 0.6 reverse_select_fusion.1
  (12 shorter events, 0.1 us)
Async XLA Ops:
  17.4 21.4 %copy-start.5 = (bf16[64,464]{1,0:T(8,128)(2,1)S(1)}, bf16[64,464]{1,0:T(8,128)(2,1)}, u32[]{:S(2)}) copy-start(bf16[64,464]{1,0:T(8,128)(2,1)} %param.6) | copy-start | bytes 178180
  35.3 15.0 %all-to-all-start.2 = ((bf16[4,4,16,1856]{3,2,1,0:T(8,128)(2,1)}), bf16[4,4,16,1856]{3,2,1,0:T(8,128)(2,1)S(1)}, u32[]{:S(2)}, u32[]{:S(2)}) async-start(bf16[4,4,16,1856]{3,2,1,0:T(8,128)(2,1)} %broadcast_in_dim.15), calls=%async_computation.2 | async-start | bytes 1966080 | tf_op jit(solution)/shard_map/all_to_all | solution.py:21
  51.0 26.5 %all-to-all-start.5 = ((bf16[4,2,32,464]{3,2,1,0:T(8,128)(2,1)}), bf16[4,2,32,464]{3,2,1,0:T(8,128)(2,1)S(1)}, u32[]{:S(2)}, u32[]{:S(2)}) async-start(bf16[4,2,32,464]{3,2,1,0:T(8,128)(2,1)} %broadcast_in_dim.32), calls=%async_computation.5 | async-start | bytes 524288 | tf_op jit(solution)/shard_map/all_to_all | solution.py:21
  63.0 31.1 %collective-permute-start = (bf16[4,4,16,1856]{3,2,1,0:T(8,128)(2,1)S(1)}, bf16[4,4,16,1856]{3,2,1,0:T(8,128)(2,1)}, u32[]{:S(2)}, u32[]{:S(2)}) collective-permute-start(bf16[4,4,16,1856]{3,2,1,0:T(8,128)(2,1)S(1)} %all_to_all.35), channel_id=1, source_target_pairs={{0,16},{16,0},{1,17},{17,1},{2,18},{18,2},{3,19},{19,3},{4,20},{20... | collective-permute-start | bytes 2850824 | tf_op jit(solution)/shard_map/ppermute | solution.py:45
  78.6 18.2 %copy-start.6 = (f32[1856]{0:T(1024)S(1)}, f32[1856]{0:T(1024)}, u32[]{:S(2)}) copy-start(f32[1856]{0:T(1024)} %param.9) | copy-start | bytes 22276
  78.6 14.4 %all-to-all-start.6 = ((bf16[4,4,2,32,464]{4,3,2,1,0:T(8,128)(2,1)}), bf16[4,4,2,32,464]{4,3,2,1,0:T(8,128)(2,1)S(1)}, u32[]{:S(2)}, u32[]{:S(2)}) async-start(bf16[4,4,2,32,464]{4,3,2,1,0:T(8,128)(2,1)} %broadcast_in_dim.33), calls=%async_computation.6 | async-start | bytes 2097152 | tf_op jit(solution)/shard_map/all_to_all | solution.py:21
  84.9 19.1 %collective-permute-start.1 = (bf16[4,4,16,1856]{3,2,1,0:T(8,128)(2,1)S(1)}, bf16[4,4,16,1856]{3,2,1,0:T(8,128)(2,1)}, u32[]{:S(2)}, u32[]{:S(2)}) collective-permute-start(bf16[4,4,16,1856]{3,2,1,0:T(8,128)(2,1)S(1)} %all-to-all-done.2), channel_id=1, source_target_pairs={{0,16},{16,0},{1,17},{17,1},{2,18},{18,2},{3,19},{19,3},{4,20},{20... | collective-permute-start | bytes 2850824 | tf_op jit(solution)/shard_map/ppermute | solution.py:45
  93.0 3.8 %copy-start.3 = (bf16[464,1856]{1,0:T(8,128)(2,1)S(1)}, bf16[464,1856]{1,0:T(8,128)(2,1)}, u32[]{:S(2)}) copy-start(bf16[464,1856]{1,0:T(8,128)(2,1)} %param.8) | copy-start | bytes 5167108
  95.5 1.3 copy-start
  99.1 13.3 %all-to-all-start.1 = ((bf16[4,4,2,16,464]{4,3,1,2,0:T(8,128)(2,1)}), bf16[4,4,2,16,464]{4,3,1,2,0:T(8,128)(2,1)S(1)}, u32[]{:S(2)}, u32[]{:S(2)}) async-start(bf16[4,4,2,16,464]{4,3,1,2,0:T(8,128)(2,1)} %copy.31), calls=%async_computation.1 | async-start | bytes 1048576 | tf_op jit(solution)/shard_map/all_to_all | solution.py:51
  105.4 1.3 copy-start.2
  106.7 10.5 %copy-start.1 = (bf16[8,4,16,1856]{3,2,1,0:T(8,128)(2,1)S(1)}, bf16[8,4,16,1856]{3,2,1,0:T(8,128)(2,1)}, u32[]{:S(2)}) copy-start(bf16[8,4,16,1856]{3,2,1,0:T(8,128)(2,1)} %copy-done) | copy-start | bytes 5701636
  112.4 12.2 %all-to-all-start.3 = ((bf16[4,4,2,16,464]{4,3,1,2,0:T(8,128)(2,1)}), bf16[4,4,2,16,464]{4,3,1,2,0:T(8,128)(2,1)S(1)}, u32[]{:S(2)}, u32[]{:S(2)}) async-start(bf16[4,4,2,16,464]{4,3,1,2,0:T(8,128)(2,1)} %copy.34), calls=%async_computation.3 | async-start | bytes 1048576 | tf_op jit(solution)/shard_map/all_to_all | solution.py:51
  124.5 5.7 %copy-start.4 = (bf16[464,1856]{1,0:T(8,128)(2,1)S(1)}, bf16[464,1856]{1,0:T(8,128)(2,1)}, u32[]{:S(2)}) copy-start(bf16[464,1856]{1,0:T(8,128)(2,1)} %param.8) | copy-start | bytes 5167108
  125.5 30.6 %all-to-all-start.4 = ((bf16[4,2,2,16,464]{4,3,1,2,0:T(8,128)(2,1)}), bf16[4,2,2,16,464]{4,3,1,2,0:T(8,128)(2,1)S(1)}, u32[]{:S(2)}, u32[]{:S(2)}) async-start(bf16[4,2,2,16,464]{4,3,1,2,0:T(8,128)(2,1)} %copy.36), calls=%async_computation.4 | async-start | bytes 524288 | tf_op jit(solution)/shard_map/all_to_all | solution.py:53

commit v3 on v1

v3 whole, which is shorter than its diff:
```python
import jax
import jax.numpy as jnp
from jax import lax
from jax.experimental import pallas as pl
from jax.experimental.pallas import tpu as pltpu
from jax.sharding import Mesh, PartitionSpec as P

ROW = ("y", "zl", "c")
COL = ("zh", "x")
SWAP = [(0, 1), (1, 0)]
TILE = 512
tie = lax.optimization_barrier
SMEM = pl.BlockSpec(memory_space=pltpu.SMEM)
VMEM = pl.BlockSpec(memory_space=pltpu.VMEM)
CONTRACT_LAST = (((1,), (1,)), ((), ()))
CONTRACT_FIRST = (((0,), (0,)), ((), ()))


def own_rows_kernel(bounds, own, w, steps, quantized, out):
    step = steps[...]
    ratio = w[...].astype(jnp.float32) * (1.0 / step)
    levels = jnp.clip(jnp.floor(ratio + 0.5), bounds[0], bounds[1])
    quantized[...] = (levels * step).astype(jnp.bfloat16)
    rows = own[...].reshape(512, own.shape[-1])
    out[...] = lax.dot_general(
        rows, quantized[...], CONTRACT_LAST, preferred_element_type=jnp.float32
    ).astype(jnp.bfloat16)


def own_rows(bounds, own, weight, steps):
    features, channels = weight.shape
    return pl.pallas_call(
        own_rows_kernel,
        out_shape=(
            jax.ShapeDtypeStruct(weight.shape, jnp.bfloat16),
            jax.ShapeDtypeStruct((512, features), jnp.bfloat16),
        ),
        in_specs=[SMEM, VMEM, VMEM, VMEM],
        out_specs=(VMEM, VMEM),
        compiler_params=pltpu.CompilerParams(vmem_limit_bytes=60 << 20),
        cost_estimate=pl.CostEstimate(
            flops=2 * 512 * features * channels,
            bytes_accessed=2 * (2 * features * channels + 512 * (features + channels)),
            transcendentals=0,
        ),
    )(bounds, own, weight, steps)


def all_rows_kernel(place, mine, other, quantized, out):
    rows = other[...].reshape(512, other.shape[-1])
    part = lax.dot_general(
        rows, quantized[...], CONTRACT_LAST, preferred_element_type=jnp.float32
    ).astype(jnp.bfloat16)
    core = place[1]
    at_mine = pl.multiple_of(core * 32, 32)
    at_other = pl.multiple_of((1 - core) * 32, 32)
    for y in range(4):
        for z in range(4):
            at = 32 * (4 * y + z)
            out[z, y, pl.ds(at_mine, 32), :] = mine[at : at + 32, :]
            out[z, y, pl.ds(at_other, 32), :] = part[at : at + 32]


def all_rows(place, mine, other, quantized):
    features, channels = quantized.shape
    return pl.pallas_call(
        all_rows_kernel,
        out_shape=jax.ShapeDtypeStruct((4, 4, 64, features), jnp.bfloat16),
        in_specs=[SMEM, VMEM, VMEM, VMEM],
        out_specs=VMEM,
        compiler_params=pltpu.CompilerParams(vmem_limit_bytes=60 << 20),
        cost_estimate=pl.CostEstimate(
            flops=2 * 512 * features * channels,
            bytes_accessed=2 * (features * channels + 512 * (4 * features + channels)),
            transcendentals=0,
        ),
    )(place, mine, other, quantized)


def weight_kernel(place, bounds, act, own, other, w, steps, out, sums, rows):
    core = place[1]

    @pl.when(pl.program_id(0) == 0)
    def _():
        for o in range(2):
            start = pl.multiple_of(jnp.abs(o - core) * 32, 32)
            for y in range(4):
                for z in range(4):
                    at = 512 * o + 32 * (4 * y + z)
                    rows[at : at + 32, :] = act[z, y, pl.ds(start, 32), :]

    grads = jnp.concatenate([own[...].reshape(512, TILE), other[...].reshape(512, TILE)], axis=0)
    wgrad = lax.dot_general(rows[...], grads, CONTRACT_FIRST, preferred_element_type=jnp.float32)
    low, high = bounds[0], bounds[1]
    ratio = w[...].astype(jnp.float32) * (1.0 / steps[...])
    levels = jnp.clip(jnp.floor(ratio + 0.5), low, high)
    inside = jnp.logical_and(ratio >= low, ratio <= high)
    out[...] = jnp.where(inside, wgrad, 0.0).astype(jnp.bfloat16)
    coefficient = jnp.where(inside, levels - ratio, levels)
    sums[...] = jnp.sum(wgrad * coefficient, axis=0, keepdims=True)


def weight_and_step_sums(place, bounds, act, own, other, weight, steps):
    features, channels = weight.shape
    column = lambda rows: pl.BlockSpec((rows, TILE), lambda j: (0, j))
    block = pl.BlockSpec((4, 4, 32, TILE), lambda j: (0, 0, 0, j))
    return pl.pallas_call(
        weight_kernel,
        grid=(pl.cdiv(channels, TILE),),
        out_shape=(
            jax.ShapeDtypeStruct(weight.shape, jnp.bfloat16),
            jax.ShapeDtypeStruct((1, channels), jnp.float32),
        ),
        in_specs=[SMEM, SMEM, pl.BlockSpec(act.shape, lambda j: (0, 0, 0, 0)), block, block]
        + [column(features), column(1)],
        out_specs=(column(features), column(1)),
        scratch_shapes=[pltpu.VMEM((1024, features), jnp.bfloat16)],
        compiler_params=pltpu.CompilerParams(vmem_limit_bytes=60 << 20),
        cost_estimate=pl.CostEstimate(
            flops=2 * 1024 * features * channels,
            bytes_accessed=2 * (2 * features * channels + 1024 * (features + channels)),
            transcendentals=0,
        ),
    )(place, bounds, act, own, other, weight, steps)


def gather(block, axis):
    return lax.all_to_all(jnp.broadcast_to(block[None], (4, *block.shape)), axis, 0, 0)


def shards(activations, output_grads, weight, step_sizes, level_low, level_high):
    f32, bf16 = jnp.float32, jnp.bfloat16
    features, channels = weight.shape
    high = level_high[0].astype(f32)
    bounds = jnp.stack([level_low[0].astype(f32), high])
    steps = step_sizes[None, :]
    place = jnp.stack([lax.axis_index(a) for a in ("y", "c", "zh", "x")]).astype(jnp.int32)

    grads = gather(output_grads, "zl")
    grads, activations = tie((grads, activations))

    own = gather(grads, "y")
    act = lax.all_gather(activations, "zh", axis=0)
    own, act = tie((own, act))

    act = gather(act, "x")
    other = lax.ppermute(own, "c", SWAP)
    quantized, mine = own_rows(bounds, own, weight, steps)
    sums = all_rows(place, mine, other, quantized)
    sums, act = tie((sums, act))

    sums = lax.all_to_all(sums, "x", 0, 0)
    sums = jnp.sum(sums.astype(f32), axis=0).astype(bf16)
    weight_grads, local = weight_and_step_sums(place, bounds, act, own, other, weight, steps)
    total = lax.psum(lax.psum(local[0], "c"), "zl")
    sums, total, weight_grads = tie((sums, total, weight_grads))

    sums = lax.all_to_all(sums, "zh", 0, 0)
    input_grads = jnp.sum(sums.astype(f32), axis=0).astype(bf16)
    scale = 1.0 / jnp.sqrt(f32(features * 32) * high)
    total = lax.psum(total, "y")
    return (input_grads, weight_grads, total * scale)


def solution(mesh):
    fine = Mesh(mesh.devices.reshape(4, 4, 2, 4, 4), ROW + COL)
    placed = (P(COL, ROW), P(ROW, COL), P(ROW, COL), P(COL), P(), P())
    return jax.shard_map(
        shards,
        mesh=fine,
        in_specs=placed,
        out_specs=(P(COL, ROW), P(ROW, COL), P(COL)),
        check_vma=False,
    )
```

time: 158 us -> 131 us (0.83)
  the two profiles are of different devices: /device:TPU:2 before, /device:TPU:36 now
where the time goes in v3:
time: 131 us
  blocking collectives  65.7 us (50%)
  starting transfers between devices  27.8 us (21%)
  Pallas kernels  16 us (12%)
  waiting for transfers between devices  10.8 us (8%)
  other arithmetic  4.18 us (3%)
  local copies, waits for them, and re-layouts  4.08 us (3%)
  between operations  2.04 us (2%)
    all_gather x1, blocking collectives, shards(): act = lax.all_gather(activations, 'zh', axis=0)  26 us
    all_to_all x1, blocking collectives, gather(): lax.all_to_all(jnp.broadcast_to(block[None], (4, *block.shape)), axis, 0, 0)  17.9 us
    psum x2, blocking collectives, shards(): total = lax.psum(lax.psum(local[0], 'c'), 'zl')  12.8 us
    all_to_all x1, waiting for transfers between devices, shards(): sums = lax.all_to_all(sums, 'zh', 0, 0)  10.2 us
    all_to_all x1, starting transfers between devices, shards(): sums = lax.all_to_all(sums, 'zh', 0, 0)  10.1 us
    all_to_all x2, starting transfers between devices, gather(): lax.all_to_all(jnp.broadcast_to(block[None], (4, *block.shape)), axis, 0, 0)  9.39 us
    psum x1, blocking collectives, shards(): total = lax.psum(total, 'y')  9.02 us
    pallas_call x1, Pallas kernels, weight_and_step_sums(): pl.pallas_call(weight_kernel, grid=(pl.cdiv(channels, TILE),), out_shape=...  6.98 us
  transfers between devices with their start and end apart: 5, of which 2 were waited for; matrix products, arithmetic and copies ran while one was open for 3% of the time, Pallas kernels for 12%

profile of v3, /device:TPU:36, one launch (start us, length us, event | category | flops | bytes accessed | tf_op | source)
XLA Modules:
  0.0 130.6 jit_solution(18009538921876167741)
XLA Ops:
  0.6 0.9 broadcast_in_dim.8
  1.6 17.9 %all_to_all.25 = bf16[4,32,1856]{2,1,0:T(8,128)(2,1)S(1)} all-to-all(bf16[4,32,1856]{2,1,0:T(8,128)(2,1)S(1)} %broadcast_in_dim.8), channel_id=1, replica_groups=mesh['y'=4,'zl'=4,'c'=2,'zh'=4,'x'=4] {'zl'}, dimensions={0} | all-to-all | bytes 950272 | tf_op jit(solution)/shard_map/all_to_all | solution.py:128
  19.4 1.4 %broadcast_in_dim.9 = bf16[4,4,32,1856]{3,2,1,0:T(8,128)(2,1)} broadcast(bf16[4,32,1856]{2,1,0:T(8,128)(2,1)S(1)} %all_to_all.25), dimensions={1,2,3} | broadcast | bytes 2375680 | tf_op jit(solution)/shard_map/broadcast_in_dim | solution.py:128
  20.9 0.0 copy-start.2
  20.9 4.6 %all-to-all-start.1 = ((bf16[4,4,32,1856]{3,2,1,0:T(8,128)(2,1)}), bf16[4,4,32,1856]{3,2,1,0:T(8,128)(2,1)S(1)}, u32[]{:S(2)}, u32[]{:S(2)}) async-start(bf16[4,4,32,1856]{3,2,1,0:T(8,128)(2,1)} %broadcast_in_dim.9), calls=%async_computation.1 | async-start | bytes 3932160 | tf_op jit(solution)/shard_map/all_to_all | solution.py:128
  25.5 0.0 copy-done.2
  25.5 0.0 copy-start.3
  25.5 26.0 %all-gather = bf16[256,464]{1,0:T(8,128)(2,1)S(1)} all-gather(bf16[64,464]{1,0:T(8,128)(2,1)S(1)} %copy-done.2), channel_id=2, replica_groups=mesh['y'=4,'zl'=4,'c'=2,'zh'=4,'x'=4] {'zh'}, dimensions={0}, use_global_device_ids=true | all-gather | bytes 296960 | tf_op jit(solution)/shard_map/all_gather | solution.py:143
  51.5 0.0 all-to-all-done.1.own
  51.5 0.0 copy-start
  51.5 1.9 %collective-permute-start = (bf16[4,4,32,1856]{3,2,1,0:T(8,128)(2,1)S(1)}, bf16[4,4,32,1856]{3,2,1,0:T(8,128)(2,1)}, u32[]{:S(2)}, u32[]{:S(2)}) collective-permute-start(bf16[4,4,32,1856]{3,2,1,0:T(8,128)(2,1)S(1)} %all-to-all-done.1.own), channel_id=1, source_target_pairs={{0,16},{16,0},{1,17},{17,1},{2,18},{18,2},{3,19},{19,3},{4,20},{20... | collective-permute-start | bytes 5701640 | tf_op jit(solution)/shard_map/ppermute | solution.py:147
  53.4 1.1 broadcast_in_dim.11
  54.5 4.8 %all-to-all-start.2 = ((bf16[4,4,64,464]{3,2,1,0:T(8,128)(2,1)}), bf16[4,4,64,464]{3,2,1,0:T(8,128)(2,1)S(1)}, u32[]{:S(2)}, u32[]{:S(2)}) async-start(bf16[4,4,64,464]{3,2,1,0:T(8,128)(2,1)} %broadcast_in_dim.11), calls=%async_computation.2 | async-start | bytes 2097152 | tf_op jit(solution)/shard_map/all_to_all | solution.py:128
  60.6 0.0 copy-done.3
  60.6 0.6 broadcast_in_dim.10.steps
  61.2 0.6 pad_maximum_fusion.bounds
  61.8 0.6 pad_add_fusion.place
  62.4 0.0 copy-done
  62.4 4.5 %shard_map.85 = (bf16[464,1856]{1,0:T(8,128)(2,1)}, bf16[512,464]{1,0:T(8,128)(2,1)}) custom-call(f32[2]{0:T(128)} %pad_maximum_fusion.bounds, bf16[4,4,32,1856]{3,2,1,0:T(8,128)(2,1)} %copy-done, bf16[464,1856]{1,0:T(8,128)(2,1)} %w.3, f32[1,1856]{1,0:T(1,128)} %broadcast_in_dim.10.steps), custom_call_target="tpu_custom_call" | custom-call | flops 881852416 | bytes 5820416 | tf_op jit(solution)/shard_map/pallas_call | solution.py:32
  67.0 0.0 collective-permute-done.other
  67.0 4.5 %shard_map.86 = bf16[4,4,64,464]{3,2,1,0:T(8,128)(2,1)} custom-call(s32[4]{0:T(128)} %pad_add_fusion.place, bf16[512,464]{1,0:T(8,128)(2,1)} %get-tuple-element.19.mine, bf16[4,4,32,1856]{3,2,1,0:T(8,128)(2,1)} %collective-permute-done.other, bf16[464,1856]{1,0:T(8,128)(2,1)} %get-tuple-element.20.quantized), custom_call_target="tpu_custom_call" | custom-call | flops 881852416 | bytes 5523456 | tf_op jit(solution)/shard_map/pallas_call | solution.py:66
  71.5 0.6 all-to-all-done.2.act
  72.1 0.0 copy-start.1
  72.1 6.5 %all-to-all-start.3 = ((bf16[4,4,64,464]{3,2,1,0:T(8,128)(2,1)}), bf16[4,4,64,464]{3,2,1,0:T(8,128)(2,1)S(1)}, u32[]{:S(2)}, u32[]{:S(2)}) async-start(bf16[4,4,64,464]{3,2,1,0:T(8,128)(2,1)} %shard_map.86), calls=%async_computation.3 | async-start | bytes 2097152 | tf_op jit(solution)/shard_map/all_to_all | solution.py:152
  78.5 0.0 copy-done.1
  78.5 7.0 %shard_map.87 = (bf16[464,1856]{1,0:T(8,128)(2,1)}, f32[1,1856]{1,0:T(1,128)}) custom-call(s32[4]{0:T(128)} %pad_add_fusion.place, f32[2]{0:T(128)} %pad_maximum_fusion.bounds, bf16[4,4,64,464]{3,2,1,0:T(8,128)(2,1)} %copy-done.1, bf16[4,4,32,1856]{3,2,1,0:T(8,128)(2,1)} %copy-done, bf16[4,4,32,1856]{3,2,1,0:T(8,128)(2,1)} %collective-permute-done.other, ...), custom_call_target="tpu_custom_call" | custom-call | flops 1763704832 | bytes 8196096 | tf_op jit(solution)/shard_map/pallas_call | solution.py:107
  85.5 0.7 reduce.2
  86.2 2.5 %psum.21 = f32[1856]{0:T(1024)S(1)} all-reduce(f32[1856]{0:T(1024)S(1)} %reduce.2), channel_id=1, replica_groups=mesh['y'=4,'zl'=4,'c'=2,'zh'=4,'x'=4] {'c'}, use_global_device_ids=true, to_apply=%region_1.0 | all-reduce | flops 1856 | bytes 14848 | tf_op jit(solution)/shard_map/psum | solution.py:155
  88.7 10.3 %psum.22 = f32[1856]{0:T(1024)S(1)} all-reduce(f32[1856]{0:T(1024)S(1)} %psum.21), channel_id=1, replica_groups=mesh['y'=4,'zl'=4,'c'=2,'zh'=4,'x'=4] {'zl'}, use_global_device_ids=true, to_apply=%region_2.0 | all-reduce | flops 1856 | bytes 14848 | tf_op jit(solution)/shard_map/psum | solution.py:155
  99.0 0.0 all-to-all-done.3
  99.0 0.9 reduce_sum.24
  100.0 10.1 %all-to-all-start.4 = ((bf16[4,64,464]{2,1,0:T(8,128)(2,1)}), bf16[4,64,464]{2,1,0:T(8,128)(2,1)S(1)}, u32[]{:S(2)}, u32[]{:S(2)}) async-start(bf16[4,64,464]{2,1,0:T(8,128)(2,1)} %reduce_sum.24), calls=%async_computation.4 | async-start | bytes 524288 | tf_op jit(solution)/shard_map/all_to_all | solution.py:158
  110.1 9.0 %psum.23 = f32[1856]{0:T(1024)S(1)} all-reduce(f32[1856]{0:T(1024)S(1)} %psum.22), channel_id=1, replica_groups=mesh['y'=4,'zl'=4,'c'=2,'zh'=4,'x'=4] {'y'}, use_global_device_ids=true, to_apply=%region_4.0 | all-reduce | flops 1856 | bytes 14848 | tf_op jit(solution)/shard_map/psum | solution.py:161
  119.1 0.6 broadcast_multiply_fusion
  119.7 10.2 %all-to-all-done.4 = bf16[4,64,464]{2,1,0:T(8,128)(2,1)S(1)} async-done(((bf16[4,64,464]{2,1,0:T(8,128)(2,1)}), bf16[4,64,464]{2,1,0:T(8,128)(2,1)S(1)}, u32[]{:S(2)}, u32[]{:S(2)}) %all-to-all-start.4) | async-done | bytes 237600 | tf_op jit(solution)/shard_map/all_to_all | solution.py:158
  129.9 0.7 reduce_sum.25
Async XLA Ops:
  20.9 4.6 %copy-start.2 = (bf16[64,464]{1,0:T(8,128)(2,1)S(1)}, bf16[64,464]{1,0:T(8,128)(2,1)}, u32[]{:S(2)}) copy-start(bf16[64,464]{1,0:T(8,128)(2,1)} %param.6) | copy-start | bytes 178180
  20.9 30.6 %all-to-all-start.1 = ((bf16[4,4,32,1856]{3,2,1,0:T(8,128)(2,1)}), bf16[4,4,32,1856]{3,2,1,0:T(8,128)(2,1)S(1)}, u32[]{:S(2)}, u32[]{:S(2)}) async-start(bf16[4,4,32,1856]{3,2,1,0:T(8,128)(2,1)} %broadcast_in_dim.9), calls=%async_computation.1 | async-start | bytes 3932160 | tf_op jit(solution)/shard_map/all_to_all | solution.py:128
  25.5 35.1 %copy-start.3 = (f32[1856]{0:T(1024)S(1)}, f32[1856]{0:T(1024)}, u32[]{:S(2)}) copy-start(f32[1856]{0:T(1024)} %param.9) | copy-start | bytes 22276
  51.5 11.0 %copy-start = (bf16[4,4,32,1856]{3,2,1,0:T(8,128)(2,1)}, bf16[4,4,32,1856]{3,2,1,0:T(8,128)(2,1)S(1)}, u32[]{:S(2)}) copy-start(bf16[4,4,32,1856]{3,2,1,0:T(8,128)(2,1)S(1)} %all-to-all-done.1.own) | copy-start | bytes 5701636
  51.5 15.5 %collective-permute-start = (bf16[4,4,32,1856]{3,2,1,0:T(8,128)(2,1)S(1)}, bf16[4,4,32,1856]{3,2,1,0:T(8,128)(2,1)}, u32[]{:S(2)}, u32[]{:S(2)}) collective-permute-start(bf16[4,4,32,1856]{3,2,1,0:T(8,128)(2,1)S(1)} %all-to-all-done.1.own), channel_id=1, source_target_pairs={{0,16},{16,0},{1,17},{17,1},{2,18},{18,2},{3,19},{19,3},{4,20},{20... | collective-permute-start | bytes 5701640 | tf_op jit(solution)/shard_map/ppermute | solution.py:147
  54.5 17.6 %all-to-all-start.2 = ((bf16[4,4,64,464]{3,2,1,0:T(8,128)(2,1)}), bf16[4,4,64,464]{3,2,1,0:T(8,128)(2,1)S(1)}, u32[]{:S(2)}, u32[]{:S(2)}) async-start(bf16[4,4,64,464]{3,2,1,0:T(8,128)(2,1)} %broadcast_in_dim.11), calls=%async_computation.2 | async-start | bytes 2097152 | tf_op jit(solution)/shard_map/all_to_all | solution.py:128
  72.1 6.5 %copy-start.1 = (bf16[4,4,64,464]{3,2,1,0:T(8,128)(2,1)}, bf16[4,4,64,464]{3,2,1,0:T(8,128)(2,1)S(1)}, u32[]{:S(2)}) copy-start(bf16[4,4,64,464]{3,2,1,0:T(8,128)(2,1)S(1)} %all-to-all-done.2.act) | copy-start | bytes 2850820
  72.1 27.0 %all-to-all-start.3 = ((bf16[4,4,64,464]{3,2,1,0:T(8,128)(2,1)}), bf16[4,4,64,464]{3,2,1,0:T(8,128)(2,1)S(1)}, u32[]{:S(2)}, u32[]{:S(2)}) async-start(bf16[4,4,64,464]{3,2,1,0:T(8,128)(2,1)} %shard_map.86), calls=%async_computation.3 | async-start | bytes 2097152 | tf_op jit(solution)/shard_map/all_to_all | solution.py:152
  100.0 29.9 %all-to-all-start.4 = ((bf16[4,64,464]{2,1,0:T(8,128)(2,1)}), bf16[4,64,464]{2,1,0:T(8,128)(2,1)S(1)}, u32[]{:S(2)}, u32[]{:S(2)}) async-start(bf16[4,64,464]{2,1,0:T(8,128)(2,1)} %reduce_sum.24), calls=%async_computation.4 | async-start | bytes 524288 | tf_op jit(solution)/shard_map/all_to_all | solution.py:158

commit v4 on v1

v4 whole, which is shorter than its diff:
```python
import jax
import jax.numpy as jnp
from jax import lax
from jax.experimental import pallas as pl
from jax.experimental.pallas import tpu as pltpu
from jax.sharding import Mesh, PartitionSpec as P

ROW = ("y", "zl", "c")
COL = ("zh", "x")
SWAP = [(0, 1), (1, 0)]
TILE = 512
HALVES = ((0, 256), (256, 464))
ANY = pl.BlockSpec(memory_space=pl.ANY)
SMEM = pl.BlockSpec(memory_space=pltpu.SMEM)
VMEM = pl.BlockSpec(memory_space=pltpu.VMEM)
CONTRACT_LAST = (((1,), (1,)), ((), ()))
tie = lax.optimization_barrier


def resident(array):
    return pltpu.with_memory_space_constraint(array, pltpu.VMEM)


def distant(array):
    return pltpu.with_memory_space_constraint(array, pltpu.HBM)


def quantize_kernel(low, high, w, steps, quantized):
    low, high = low[0].astype(jnp.float32), high[0].astype(jnp.float32)
    step = steps[...][None, :]
    ratio = w[...].astype(jnp.float32) * (1.0 / step)
    levels = jnp.clip(jnp.floor(ratio + 0.5), low, high)
    quantized[...] = (levels * step).astype(jnp.bfloat16)


def quantize(low, high, weight, steps):
    features, channels = weight.shape
    return pl.pallas_call(
        quantize_kernel,
        out_shape=pltpu.HBM(weight.shape, jnp.bfloat16),
        in_specs=[SMEM, SMEM, VMEM, VMEM],
        out_specs=VMEM,
        compiler_params=pltpu.CompilerParams(vmem_limit_bytes=24 << 20),
        cost_estimate=pl.CostEstimate(
            flops=10 * features * channels, bytes_accessed=4 * features * channels, transcendentals=0
        ),
    )(low, high, weight, steps)


def products_kernel(
    low, high, own, other, act, quantized_hbm, w_hbm, steps, sums_hbm, grads_hbm, local,
    quantized, w, rows, sums, grads, sems,
):
    core = lax.axis_index("c")
    at_own = pl.multiple_of(core * 32, 32)
    at_other = pl.multiple_of((1 - core) * 32, 32)
    parts = [pl.ds(top, bottom - top) for top, bottom in HALVES]
    loads = [
        pltpu.make_async_copy(quantized_hbm.at[part], quantized.at[part], sems.at[n])
        for n, part in enumerate(parts)
    ]
    loads.append(pltpu.make_async_copy(w_hbm, w, sems.at[2]))
    for load in loads:
        load.start()
    low, high = low[0].astype(jnp.float32), high[0].astype(jnp.float32)
    features, channels = w.shape
    tiles = [(a, min(a + TILE, channels)) for a in range(0, channels, TILE)]

    for (top, bottom), load in zip(HALVES, loads[:2]):
        load.wait()
        for tokens, at in ((own, at_own), (other, at_other)):
            part = lax.dot_general(
                tokens[...].reshape(512, channels),
                quantized[top:bottom, :],
                CONTRACT_LAST,
                preferred_element_type=jnp.float32,
            ).astype(jnp.bfloat16)
            for y in range(4):
                for z in range(4):
                    sums[z, y, pl.ds(at, 32), top:bottom] = part[32 * (4 * y + z) : 32 * (4 * y + z) + 32]
    stores = [pltpu.make_async_copy(sums, sums_hbm, sems.at[3])]
    stores[0].start()

    for z in range(4):
        tokens = [act[z, y, pl.ds(at, 32), :] for y in range(4) for at in (at_own, at_other)]
        rows[:, 256 * z : 256 * z + 256] = jnp.concatenate(tokens, axis=0).T

    loads[2].wait()
    scale = 1.0 / jnp.sqrt(jnp.full((1, 128), 32 * features * high, jnp.float32))
    for n, (top, bottom) in enumerate(HALVES):
        for a, b in tiles:
            blocks = [half[4 * y + z, :, a:b] for z in range(4) for y in range(4) for half in (own, other)]
            wgrad = jnp.dot(rows[top:bottom, :], jnp.concatenate(blocks, axis=0), preferred_element_type=jnp.float32)
            ratio = w[top:bottom, a:b].astype(jnp.float32) * (1.0 / steps[a:b][None, :])
            levels = jnp.clip(jnp.floor(ratio + 0.5), low, high)
            inside = jnp.logical_and(ratio >= low, ratio <= high)
            grads[top:bottom, a:b] = jnp.where(inside, wgrad, 0.0).astype(jnp.bfloat16)
            coefficient = jnp.where(inside, levels - ratio, levels)
            partial = jnp.sum(wgrad * coefficient, axis=0) * scale[0, 0]
            local[a:b] = partial if n == 0 else local[a:b] + partial
        stores.append(pltpu.make_async_copy(grads.at[parts[n]], grads_hbm.at[parts[n]], sems.at[4 + n]))
        stores[-1].start()
    for store in stores:
        store.wait()


def products(low, high, own, other, act, quantized, weight, steps):
    features, channels = weight.shape
    own, other = (tokens.reshape(16, 32, channels) for tokens in (own, other))
    bf16 = jnp.bfloat16
    return pl.pallas_call(
        products_kernel,
        out_shape=(
            pltpu.HBM((4, 4, 64, features), bf16),
            pltpu.HBM(weight.shape, bf16),
            jax.ShapeDtypeStruct((channels,), jnp.float32),
        ),
        in_specs=[SMEM, SMEM, VMEM, VMEM, VMEM, ANY, ANY, VMEM],
        out_specs=(ANY, ANY, VMEM),
        scratch_shapes=[
            pltpu.VMEM(weight.shape, bf16),
            pltpu.VMEM(weight.shape, bf16),
            pltpu.VMEM((features, 1024), bf16),
            pltpu.VMEM((4, 4, 64, features), bf16),
            pltpu.VMEM(weight.shape, bf16),
            pltpu.SemaphoreType.DMA((6,)),
        ],
        compiler_params=pltpu.CompilerParams(vmem_limit_bytes=24 << 20),
        cost_estimate=pl.CostEstimate(
            flops=4 * 1024 * features * channels,
            bytes_accessed=2 * (2 * features * channels + 1024 * (2 * features + channels)),
            transcendentals=0,
        ),
    )(low, high, *map(resident, (own, other, act)), distant(quantized), distant(weight), steps)


def gather(block, axis):
    return lax.all_to_all(jnp.broadcast_to(block[None], (4, *block.shape)), axis, 0, 0)


def shards(activations, output_grads, weight, step_sizes, level_low, level_high):
    f32, bf16 = jnp.float32, jnp.bfloat16

    grads = gather(output_grads, "zl")
    act = lax.all_gather(activations, "zh", axis=0)
    grads, act = tie((grads, act))

    own = gather(grads, "y")
    act = lax.all_gather(act, "x", axis=0)
    quantized = quantize(level_low, level_high, weight, step_sizes)
    own, act, quantized = tie((own, act, quantized))

    other = lax.ppermute(own, "c", SWAP)
    sums, weight_grads, total = products(level_low, level_high, own, other, act, quantized, weight, step_sizes)

    sums = lax.all_to_all(sums, "x", 0, 0)
    sums = jnp.sum(sums.astype(f32), axis=0).astype(bf16)
    total = lax.psum(lax.psum(total, "c"), "zl")
    sums, total = tie((sums, total))

    sums = lax.all_to_all(sums, "zh", 0, 0)
    input_grads = jnp.sum(sums.astype(f32), axis=0).astype(bf16)
    return (input_grads, weight_grads, lax.psum(total, "y"))


def solution(mesh):
    fine = Mesh(mesh.devices.reshape(4, 4, 2, 4, 4), ROW + COL)
    placed = (P(COL, ROW), P(ROW, COL), P(ROW, COL), P(COL), P(), P())
    return jax.shard_map(
        shards,
        mesh=fine,
        in_specs=placed,
        out_specs=(P(COL, ROW), P(ROW, COL), P(COL)),
        check_vma=False,
    )
```

time: 158 us -> 129 us (0.82)
  the two profiles are of different devices: /device:TPU:2 before, /device:TPU:32 now
where the time goes in v4:
time: 129 us; the launch traced here: 128 us
  blocking collectives  66.8 us (52%)
  starting transfers between devices  26.3 us (20%)
  waiting for transfers between devices  17.8 us (14%)
  Pallas kernels  9.33 us (7%)
  local copies, waits for them, and re-layouts  4.64 us (4%)
  between operations  1.98 us (2%)
  other arithmetic  1.6 us (1%)
    all_gather x1, blocking collectives, shards(): act = lax.all_gather(activations, 'zh', axis=0)  29.3 us
    all_gather x1, blocking collectives, shards(): act = lax.all_gather(act, 'x', axis=0)  15.5 us
    all_to_all x2, starting transfers between devices, gather(): lax.all_to_all(jnp.broadcast_to(block[None], (4, *block.shape)), axis, 0, 0)  13.5 us
    psum x2, blocking collectives, shards(): total = lax.psum(lax.psum(total, 'c'), 'zl')  12.4 us
    psum x1, blocking collectives, shards(): return (input_grads, weight_grads, lax.psum(total, 'y'))  9.55 us
    all_to_all x1, waiting for transfers between devices, shards(): sums = lax.all_to_all(sums, 'zh', 0, 0)  9.19 us
    pallas_call x1, Pallas kernels, products(): pl.pallas_call(products_kernel, out_shape=(pltpu.HBM((4, 4, 64, features)...  7.26 us
    all_to_all x1, starting transfers between devices, shards(): sums = lax.all_to_all(sums, 'zh', 0, 0)  6.53 us
  transfers between devices with their start and end apart: 5, of which 4 were waited for; matrix products, arithmetic and copies ran while one was open for 0% of the time, Pallas kernels for 2%

profile of v4, /device:TPU:32, one launch (start us, length us, event | category | flops | bytes accessed | tf_op | source)
XLA Modules:
  0.0 128.4 jit_solution(16837680099980521600)
XLA Ops:
  0.6 1.7 %broadcast_in_dim.4 = bf16[4,32,1856]{2,1,0:T(8,128)(2,1)} broadcast(bf16[32,1856]{1,0:T(8,128)(2,1)} %param.7), dimensions={1,2} | broadcast | bytes 593920 | tf_op jit(solution)/shard_map/broadcast_in_dim | solution.py:138
  2.3 8.9 %all-to-all-start = ((bf16[4,32,1856]{2,1,0:T(8,128)(2,1)}), bf16[4,32,1856]{2,1,0:T(8,128)(2,1)S(1)}, u32[]{:S(2)}, u32[]{:S(2)}) async-start(bf16[4,32,1856]{2,1,0:T(8,128)(2,1)} %broadcast_in_dim.4), calls=%async_computation | async-start | bytes 983040 | tf_op jit(solution)/shard_map/all_to_all | solution.py:138
  11.3 29.3 %all-gather = bf16[256,464]{1,0:T(8,128)(2,1)S(1)} all-gather(bf16[64,464]{1,0:T(8,128)(2,1)} %param.6), channel_id=2, replica_groups=mesh['y'=4,'zl'=4,'c'=2,'zh'=4,'x'=4] {'zh'}, dimensions={0}, use_global_device_ids=true | all-gather | bytes 296960 | tf_op jit(solution)/shard_map/all_gather | solution.py:145
  40.5 0.0 all-to-all-done
  40.5 1.4 %broadcast_in_dim.5 = bf16[4,4,32,1856]{3,2,1,0:T(8,128)(2,1)} broadcast(bf16[4,32,1856]{2,1,0:T(8,128)(2,1)S(1)} %all-to-all-done), dimensions={1,2,3} | broadcast | bytes 2375680 | tf_op jit(solution)/shard_map/broadcast_in_dim | solution.py:138
  42.0 0.0 copy-start.1
  42.0 4.6 %all-to-all-start.1 = ((bf16[4,4,32,1856]{3,2,1,0:T(8,128)(2,1)}), bf16[4,4,32,1856]{3,2,1,0:T(8,128)(2,1)S(1)}, u32[]{:S(2)}, u32[]{:S(2)}) async-start(bf16[4,4,32,1856]{3,2,1,0:T(8,128)(2,1)} %broadcast_in_dim.5), calls=%async_computation.1 | async-start | bytes 3932160 | tf_op jit(solution)/shard_map/all_to_all | solution.py:138
  47.9 0.0 copy-done.1
  47.9 0.0 copy-start
  47.9 1.5 %copy-done = bf16[464,1856]{1,0:T(8,128)(2,1)S(1)} copy-done((bf16[464,1856]{1,0:T(8,128)(2,1)S(1)}, bf16[464,1856]{1,0:T(8,128)(2,1)}, u32[]{:S(2)}) %copy-start) | copy-done | bytes 1722392
  49.4 2.1 %shard_map.85.quantized_hbm = bf16[464,1856]{1,0:T(8,128)(2,1)} custom-call(s32[1]{0:T(128)S(6)} %copy.9.low, s32[1]{0:T(128)S(6)} %copy.10.high, bf16[464,1856]{1,0:T(8,128)(2,1)S(1)} %copy-done, f32[1856]{0:T(1024)S(1)} %copy-done.1), custom_call_target="tpu_custom_call" | custom-call | flops 8611840 | bytes 3444736 | tf_op jit(solution)/shard_map/pallas_call | solution.py:38
  51.5 15.5 %all-gather.1 = bf16[16,64,464]{2,1,0:T(8,128)(2,1)S(1)} all-gather(bf16[4,64,464]{2,1,0:T(8,128)(2,1)S(1)} %bitcast.7), channel_id=3, replica_groups=mesh['y'=4,'zl'=4,'c'=2,'zh'=4,'x'=4] {'x'}, dimensions={0}, use_global_device_ids=true | all-gather | bytes 1187840 | tf_op jit(solution)/shard_map/all_gather | solution.py:149
  67.0 1.7 %all-to-all-done.1 = bf16[4,4,32,1856]{3,2,1,0:T(8,128)(2,1)S(1)} async-done(((bf16[4,4,32,1856]{3,2,1,0:T(8,128)(2,1)}), bf16[4,4,32,1856]{3,2,1,0:T(8,128)(2,1)S(1)}, u32[]{:S(2)}, u32[]{:S(2)}) %all-to-all-start.1) | async-done | bytes 1900576 | tf_op jit(solution)/shard_map/all_to_all | solution.py:138
  68.7 1.9 %collective-permute-start = (bf16[4,4,32,1856]{3,2,1,0:T(8,128)(2,1)S(1)}, bf16[4,4,32,1856]{3,2,1,0:T(8,128)(2,1)S(1)}, u32[]{:S(2)}, u32[]{:S(2)}) collective-permute-start(bf16[4,4,32,1856]{3,2,1,0:T(8,128)(2,1)S(1)} %all-to-all-done.1), channel_id=1, source_target_pairs={{0,16},{16,0},{1,17},{17,1},{2,18},{18,2},{3,19},{19,3},{4,20},{20... | collective-permute-start | bytes 5701640 | tf_op jit(solution)/shard_map/ppermute | solution.py:153
  70.6 3.9 %collective-permute-done = bf16[4,4,32,1856]{3,2,1,0:T(8,128)(2,1)S(1)} collective-permute-done((bf16[4,4,32,1856]{3,2,1,0:T(8,128)(2,1)S(1)}, bf16[4,4,32,1856]{3,2,1,0:T(8,128)(2,1)S(1)}, u32[]{:S(2)}, u32[]{:S(2)}) %collective-permute-start) | collective-permute-done | bytes 1900576 | tf_op jit(solution)/shard_map/ppermute | solution.py:153
  74.6 7.3 %shard_map.86 = (bf16[4,4,64,464]{3,2,1,0:T(8,128)(2,1)}, bf16[464,1856]{1,0:T(8,128)(2,1)}, f32[1856]{0:T(1024)S(1)}) custom-call(s32[1]{0:T(128)S(6)} %copy.9.low, s32[1]{0:T(128)S(6)} %copy.10.high, bf16[16,32,1856]{2,1,0:T(8,128)(2,1)S(1)} %bitcast.4, bf16[16,32,1856]{2,1,0:T(8,128)(2,1)S(1)} %bitcast.6, bf16[4,4,64,464]{3,2,1,0:T(8,128)(2,1)S(1)} %bitcast.5, ...), custom_call_target="tpu_custom_call" | custom-call | flops 3527409664 | bytes 9146368 | tf_op jit(solution)/shard_map/pallas_call | solution.py:111
  81.8 4.3 %all-to-all-start.2 = ((bf16[4,4,64,464]{3,2,1,0:T(8,128)(2,1)}), bf16[4,4,64,464]{3,2,1,0:T(8,128)(2,1)S(1)}, u32[]{:S(2)}, u32[]{:S(2)}) async-start(bf16[4,4,64,464]{3,2,1,0:T(8,128)(2,1)} %get-tuple-element.18), calls=%async_computation.2 | async-start | bytes 2097152 | tf_op jit(solution)/shard_map/all_to_all | solution.py:156
  86.1 2.5 %psum.21 = f32[1856]{0:T(1024)S(1)} all-reduce(f32[1856]{0:T(1024)S(1)} %get-tuple-element.19), channel_id=1, replica_groups=mesh['y'=4,'zl'=4,'c'=2,'zh'=4,'x'=4] {'c'}, use_global_device_ids=true, to_apply=%region_1.0 | all-reduce | flops 1856 | bytes 14848 | tf_op jit(solution)/shard_map/psum | solution.py:158
  88.6 10.0 %psum.22 = f32[1856]{0:T(1024)S(1)} all-reduce(f32[1856]{0:T(1024)S(1)} %psum.21), channel_id=1, replica_groups=mesh['y'=4,'zl'=4,'c'=2,'zh'=4,'x'=4] {'zl'}, use_global_device_ids=true, to_apply=%region_2.0 | all-reduce | flops 1856 | bytes 14848 | tf_op jit(solution)/shard_map/psum | solution.py:158
  98.6 3.0 %all-to-all-done.2 = bf16[4,4,64,464]{3,2,1,0:T(8,128)(2,1)S(1)} async-done(((bf16[4,4,64,464]{3,2,1,0:T(8,128)(2,1)}), bf16[4,4,64,464]{3,2,1,0:T(8,128)(2,1)S(1)}, u32[]{:S(2)}, u32[]{:S(2)}) %all-to-all-start.2) | async-done | bytes 950304 | tf_op jit(solution)/shard_map/all_to_all | solution.py:156
  101.5 0.9 reduce_sum.24
  102.5 6.5 %all-to-all-start.3 = ((bf16[4,64,464]{2,1,0:T(8,128)(2,1)}), bf16[4,64,464]{2,1,0:T(8,128)(2,1)S(1)}, u32[]{:S(2)}, u32[]{:S(2)}) async-start(bf16[4,64,464]{2,1,0:T(8,128)(2,1)} %reduce_sum.24), calls=%async_computation.3 | async-start | bytes 524288 | tf_op jit(solution)/shard_map/all_to_all | solution.py:161
  109.0 9.6 %psum.23 = f32[1856]{0:T(1024)} all-reduce(f32[1856]{0:T(1024)S(1)} %psum.22), channel_id=1, replica_groups=mesh['y'=4,'zl'=4,'c'=2,'zh'=4,'x'=4] {'y'}, use_global_device_ids=true, to_apply=%region_4.0 | all-reduce | flops 1856 | bytes 14848 | tf_op jit(solution)/shard_map/psum | solution.py:163
  118.5 9.2 %all-to-all-done.3 = bf16[4,64,464]{2,1,0:T(8,128)(2,1)S(1)} async-done(((bf16[4,64,464]{2,1,0:T(8,128)(2,1)}), bf16[4,64,464]{2,1,0:T(8,128)(2,1)S(1)}, u32[]{:S(2)}, u32[]{:S(2)}) %all-to-all-start.3) | async-done | bytes 237600 | tf_op jit(solution)/shard_map/all_to_all | solution.py:161
  127.7 0.7 reduce_sum.25
Async XLA Ops:
  2.3 38.2 %all-to-all-start = ((bf16[4,32,1856]{2,1,0:T(8,128)(2,1)}), bf16[4,32,1856]{2,1,0:T(8,128)(2,1)S(1)}, u32[]{:S(2)}, u32[]{:S(2)}) async-start(bf16[4,32,1856]{2,1,0:T(8,128)(2,1)} %broadcast_in_dim.4), calls=%async_computation | async-start | bytes 983040 | tf_op jit(solution)/shard_map/all_to_all | solution.py:138
  42.0 5.9 %copy-start.1 = (f32[1856]{0:T(1024)S(1)}, f32[1856]{0:T(1024)}, u32[]{:S(2)}) copy-start(f32[1856]{0:T(1024)} %steps.3) | copy-start | bytes 22276
  42.0 26.7 %all-to-all-start.1 = ((bf16[4,4,32,1856]{3,2,1,0:T(8,128)(2,1)}), bf16[4,4,32,1856]{3,2,1,0:T(8,128)(2,1)S(1)}, u32[]{:S(2)}, u32[]{:S(2)}) async-start(bf16[4,4,32,1856]{3,2,1,0:T(8,128)(2,1)} %broadcast_in_dim.5), calls=%async_computation.1 | async-start | bytes 3932160 | tf_op jit(solution)/shard_map/all_to_all | solution.py:138
  47.9 1.5 %copy-start = (bf16[464,1856]{1,0:T(8,128)(2,1)S(1)}, bf16[464,1856]{1,0:T(8,128)(2,1)}, u32[]{:S(2)}) copy-start(bf16[464,1856]{1,0:T(8,128)(2,1)} %w_hbm.1) | copy-start | bytes 5167108
  68.7 5.9 %collective-permute-start = (bf16[4,4,32,1856]{3,2,1,0:T(8,128)(2,1)S(1)}, bf16[4,4,32,1856]{3,2,1,0:T(8,128)(2,1)S(1)}, u32[]{:S(2)}, u32[]{:S(2)}) collective-permute-start(bf16[4,4,32,1856]{3,2,1,0:T(8,128)(2,1)S(1)} %all-to-all-done.1), channel_id=1, source_target_pairs={{0,16},{16,0},{1,17},{17,1},{2,18},{18,2},{3,19},{19,3},{4,20},{20... | collective-permute-start | bytes 5701640 | tf_op jit(solution)/shard_map/ppermute | solution.py:153
  81.8 19.7 %all-to-all-start.2 = ((bf16[4,4,64,464]{3,2,1,0:T(8,128)(2,1)}), bf16[4,4,64,464]{3,2,1,0:T(8,128)(2,1)S(1)}, u32[]{:S(2)}, u32[]{:S(2)}) async-start(bf16[4,4,64,464]{3,2,1,0:T(8,128)(2,1)} %get-tuple-element.18), calls=%async_computation.2 | async-start | bytes 2097152 | tf_op jit(solution)/shard_map/all_to_all | solution.py:156
  102.5 25.3 %all-to-all-start.3 = ((bf16[4,64,464]{2,1,0:T(8,128)(2,1)}), bf16[4,64,464]{2,1,0:T(8,128)(2,1)S(1)}, u32[]{:S(2)}, u32[]{:S(2)}) async-start(bf16[4,64,464]{2,1,0:T(8,128)(2,1)} %reduce_sum.24), calls=%async_computation.3 | async-start | bytes 524288 | tf_op jit(solution)/shard_map/all_to_all | solution.py:161

commit v5 on v4

v5 whole, which is shorter than its diff:
```python
import jax
import jax.numpy as jnp
from jax import lax
from jax.experimental import pallas as pl
from jax.experimental.pallas import tpu as pltpu
from jax.sharding import Mesh, PartitionSpec as P

ROW = ("y", "zl", "c")
COL = ("zh", "x")
SWAP = [(0, 1), (1, 0)]
TILE = 512
HALVES = ((0, 256), (256, 464))
ANY = pl.BlockSpec(memory_space=pl.ANY)
SMEM = pl.BlockSpec(memory_space=pltpu.SMEM)
VMEM = pl.BlockSpec(memory_space=pltpu.VMEM)
CONTRACT_LAST = (((1,), (1,)), ((), ()))
tie = lax.optimization_barrier


def resident(array):
    return pltpu.with_memory_space_constraint(array, pltpu.VMEM)


def distant(array):
    return pltpu.with_memory_space_constraint(array, pltpu.HBM)


def products_kernel(
    bounds, own, other, act, w_hbm, steps, sums_hbm, grads_hbm, local,
    quantized, w, rows, sums, grads, sems,
):
    core = lax.axis_index("c")
    at_own = pl.multiple_of(core * 32, 32)
    at_other = pl.multiple_of((1 - core) * 32, 32)
    parts = [pl.ds(top, bottom - top) for top, bottom in HALVES]
    loads = [pltpu.make_async_copy(w_hbm.at[part], w.at[part], sems.at[n]) for n, part in enumerate(parts)]
    for load in loads:
        load.start()
    low, high = bounds[0], bounds[1]
    features, channels = w.shape
    tiles = [(a, min(a + TILE, channels)) for a in range(0, channels, TILE)]

    for (top, bottom), load in zip(HALVES, loads):
        load.wait()
        for a, b in tiles:
            step = steps[a:b][None, :]
            ratio = w[top:bottom, a:b].astype(jnp.float32) * (1.0 / step)
            levels = jnp.clip(jnp.floor(ratio + 0.5), low, high)
            quantized[top:bottom, a:b] = (levels * step).astype(jnp.bfloat16)
        for tokens, at in ((own, at_own), (other, at_other)):
            part = lax.dot_general(
                tokens[...].reshape(512, channels),
                quantized[top:bottom, :],
                CONTRACT_LAST,
                preferred_element_type=jnp.float32,
            ).astype(jnp.bfloat16)
            for y in range(4):
                for z in range(4):
                    sums[z, y, pl.ds(at, 32), top:bottom] = part[32 * (4 * y + z) : 32 * (4 * y + z) + 32]
    stores = [pltpu.make_async_copy(sums, sums_hbm, sems.at[2])]
    stores[0].start()

    for z in range(4):
        tokens = [act[z, y, pl.ds(at, 32), :] for y in range(4) for at in (at_own, at_other)]
        rows[:, 256 * z : 256 * z + 256] = jnp.concatenate(tokens, axis=0).T

    scale = 1.0 / jnp.sqrt(jnp.full((1, 128), 32 * features * high, jnp.float32))
    for n, (top, bottom) in enumerate(HALVES):
        for a, b in tiles:
            blocks = [half[4 * y + z, :, a:b] for z in range(4) for y in range(4) for half in (own, other)]
            wgrad = jnp.dot(rows[top:bottom, :], jnp.concatenate(blocks, axis=0), preferred_element_type=jnp.float32)
            ratio = w[top:bottom, a:b].astype(jnp.float32) * (1.0 / steps[a:b][None, :])
            levels = jnp.clip(jnp.floor(ratio + 0.5), low, high)
            inside = jnp.logical_and(ratio >= low, ratio <= high)
            grads[top:bottom, a:b] = jnp.where(inside, wgrad, 0.0).astype(jnp.bfloat16)
            coefficient = jnp.where(inside, levels - ratio, levels)
            partial = jnp.sum(wgrad * coefficient, axis=0) * scale[0, 0]
            local[a:b] = partial if n == 0 else local[a:b] + partial
        stores.append(pltpu.make_async_copy(grads.at[parts[n]], grads_hbm.at[parts[n]], sems.at[3 + n]))
        stores[-1].start()
    for store in stores:
        store.wait()


def products(bounds, own, other, act, weight, steps):
    features, channels = weight.shape
    own, other = (tokens.reshape(16, 32, channels) for tokens in (own, other))
    bf16 = jnp.bfloat16
    return pl.pallas_call(
        products_kernel,
        out_shape=(
            pltpu.HBM((4, 4, 64, features), bf16),
            pltpu.HBM(weight.shape, bf16),
            jax.ShapeDtypeStruct((channels,), jnp.float32),
        ),
        in_specs=[SMEM, VMEM, VMEM, VMEM, ANY, VMEM],
        out_specs=(ANY, ANY, VMEM),
        scratch_shapes=[
            pltpu.VMEM(weight.shape, bf16),
            pltpu.VMEM(weight.shape, bf16),
            pltpu.VMEM((features, 1024), bf16),
            pltpu.VMEM((4, 4, 64, features), bf16),
            pltpu.VMEM(weight.shape, bf16),
            pltpu.SemaphoreType.DMA((5,)),
        ],
        compiler_params=pltpu.CompilerParams(vmem_limit_bytes=24 << 20),
        cost_estimate=pl.CostEstimate(
            flops=4 * 1024 * features * channels,
            bytes_accessed=2 * (2 * features * channels + 1024 * (2 * features + channels)),
            transcendentals=0,
        ),
    )(bounds, *map(resident, (own, other, act)), distant(weight), steps)


def gather(block, axis):
    return lax.all_to_all(jnp.broadcast_to(block[None], (4, *block.shape)), axis, 0, 0)


def shards(activations, output_grads, weight, step_sizes, level_low, level_high):
    f32, bf16 = jnp.float32, jnp.bfloat16

    grads = gather(output_grads, "zl")
    grads, activations = tie((grads, activations))

    own = gather(grads, "y")
    act = lax.all_gather(activations, "zh", axis=0)
    bounds = jnp.concatenate([level_low, level_high]).astype(f32)
    own, act, bounds = tie((own, act, bounds))

    other = lax.ppermute(own, "c", SWAP)
    act = lax.all_gather(act, "x", axis=0)
    sums, weight_grads, total = products(bounds, own, other, act, weight, step_sizes)

    sums = lax.all_to_all(sums, "x", 0, 0)
    sums = jnp.sum(sums.astype(f32), axis=0).astype(bf16)
    total = lax.psum(total, "zl")
    sums, total = tie((sums, total))

    sums = lax.all_to_all(sums, "zh", 0, 0)
    input_grads = jnp.sum(sums.astype(f32), axis=0).astype(bf16)
    return (input_grads, weight_grads, lax.psum(lax.psum(total, "y"), "c"))


def solution(mesh):
    fine = Mesh(mesh.devices.reshape(4, 4, 2, 4, 4), ROW + COL)
    placed = (P(COL, ROW), P(ROW, COL), P(ROW, COL), P(COL), P(), P())
    return jax.shard_map(
        shards,
        mesh=fine,
        in_specs=placed,
        out_specs=(P(COL, ROW), P(ROW, COL), P(COL)),
        check_vma=False,
    )
```

time: 129 us -> 126 us (0.977)
  the two profiles are of different devices: /device:TPU:32 before, /device:TPU:2 now
where the time goes in v5:
time: 126 us; the launch traced here: 125 us
  blocking collectives  82.3 us (65%)
  starting transfers between devices  19.9 us (16%)
  waiting for transfers between devices  9.37 us (7%)
  Pallas kernels  7.79 us (6%)
  local copies, waits for them, and re-layouts  2.39 us (2%)
  between operations  1.97 us (2%)
  other arithmetic  1.68 us (1%)
    all_gather x1, blocking collectives, shards(): act = lax.all_gather(activations, 'zh', axis=0)  26 us
    all_to_all x1, blocking collectives, gather(): lax.all_to_all(jnp.broadcast_to(block[None], (4, *block.shape)), axis, 0, 0)  19.5 us
    all_gather x1, blocking collectives, shards(): act = lax.all_gather(act, 'x', axis=0)  15.5 us
    psum x2, blocking collectives, shards(): return (input_grads, weight_grads, lax.psum(lax.psum(total, 'y'), 'c'))  12.1 us
    psum x1, blocking collectives, shards(): total = lax.psum(total, 'zl')  9.18 us
    all_to_all x1, starting transfers between devices, shards(): sums = lax.all_to_all(sums, 'zh', 0, 0)  8.85 us
    pallas_call x1, Pallas kernels, products(): pl.pallas_call(products_kernel, out_shape=(pltpu.HBM((4, 4, 64, features)...  7.79 us
    all_to_all x1, waiting for transfers between devices, shards(): sums = lax.all_to_all(sums, 'zh', 0, 0)  6.11 us
  transfers between devices with their start and end apart: 4, of which 2 were waited for; matrix products, arithmetic and copies ran while one was open for 0% of the time, Pallas kernels for 0%

profile of v5, /device:TPU:2, one launch (start us, length us, event | category | flops | bytes accessed | tf_op | source)
XLA Modules:
  0.0 125.4 jit_solution(12770678822186483218)
XLA Ops:
  0.6 0.9 broadcast_in_dim.4
  1.6 19.5 %all_to_all.20 = bf16[4,32,1856]{2,1,0:T(8,128)(2,1)S(1)} all-to-all(bf16[4,32,1856]{2,1,0:T(8,128)(2,1)S(1)} %broadcast_in_dim.4), channel_id=1, replica_groups=mesh['y'=4,'zl'=4,'c'=2,'zh'=4,'x'=4] {'zl'}, dimensions={0} | all-to-all | bytes 950272 | tf_op jit(solution)/shard_map/all_to_all | solution.py:116
  21.1 1.4 %broadcast_in_dim.5 = bf16[4,4,32,1856]{3,2,1,0:T(8,128)(2,1)} broadcast(bf16[4,32,1856]{2,1,0:T(8,128)(2,1)S(1)} %all_to_all.20), dimensions={1,2,3} | broadcast | bytes 2375680 | tf_op jit(solution)/shard_map/broadcast_in_dim | solution.py:116
  22.5 0.0 copy-start.1
  22.5 0.0 copy-start
  22.5 4.6 %all-to-all-start.1 = ((bf16[4,4,32,1856]{3,2,1,0:T(8,128)(2,1)}), bf16[4,4,32,1856]{3,2,1,0:T(8,128)(2,1)S(1)}, u32[]{:S(2)}, u32[]{:S(2)}) async-start(bf16[4,4,32,1856]{3,2,1,0:T(8,128)(2,1)} %broadcast_in_dim.5), calls=%async_computation.1 | async-start | bytes 3932160 | tf_op jit(solution)/shard_map/all_to_all | solution.py:116
  28.4 0.1 add_convert_fusion.bounds
  28.5 0.0 copy-done.1
  28.5 26.0 %all-gather = bf16[256,464]{1,0:T(8,128)(2,1)S(1)} all-gather(bf16[64,464]{1,0:T(8,128)(2,1)S(1)} %copy-done.1), channel_id=2, replica_groups=mesh['y'=4,'zl'=4,'c'=2,'zh'=4,'x'=4] {'zh'}, dimensions={0}, use_global_device_ids=true | all-gather | bytes 296960 | tf_op jit(solution)/shard_map/all_gather | solution.py:126
  54.5 0.0 all-to-all-done.1
  54.5 1.9 %collective-permute-start = (bf16[4,4,32,1856]{3,2,1,0:T(8,128)(2,1)S(1)}, bf16[4,4,32,1856]{3,2,1,0:T(8,128)(2,1)S(1)}, u32[]{:S(2)}, u32[]{:S(2)}) collective-permute-start(bf16[4,4,32,1856]{3,2,1,0:T(8,128)(2,1)S(1)} %all-to-all-done.1), channel_id=1, source_target_pairs={{0,16},{16,0},{1,17},{17,1},{2,18},{18,2},{3,19},{19,3},{4,20},{20... | collective-permute-start | bytes 5701640 | tf_op jit(solution)/shard_map/ppermute | solution.py:130
  56.4 15.5 %all-gather.1 = bf16[16,64,464]{2,1,0:T(8,128)(2,1)S(1)} all-gather(bf16[4,64,464]{2,1,0:T(8,128)(2,1)S(1)} %bitcast.7), channel_id=3, replica_groups=mesh['y'=4,'zl'=4,'c'=2,'zh'=4,'x'=4] {'x'}, dimensions={0}, use_global_device_ids=true | all-gather | bytes 1187840 | tf_op jit(solution)/shard_map/all_gather | solution.py:131
  71.9 0.0 collective-permute-done
  71.9 0.0 copy-done
  71.9 7.8 %shard_map.85 = (bf16[4,4,64,464]{3,2,1,0:T(8,128)(2,1)}, bf16[464,1856]{1,0:T(8,128)(2,1)}, f32[1856]{0:T(1024)S(1)}) custom-call(f32[2]{0:T(128)S(1)} %add_convert_fusion.bounds, bf16[16,32,1856]{2,1,0:T(8,128)(2,1)S(1)} %bitcast.4, bf16[16,32,1856]{2,1,0:T(8,128)(2,1)S(1)} %bitcast.6, bf16[4,4,64,464]{3,2,1,0:T(8,128)(2,1)S(1)} %bitcast.5, ...), custom_call_target="tpu_custom_call" | custom-call | flops 3527409664 | bytes 9146368 | tf_op jit(solution)/shard_map/pallas_call | solution.py:89
  79.7 4.5 %all-to-all-start.2 = ((bf16[4,4,64,464]{3,2,1,0:T(8,128)(2,1)}), bf16[4,4,64,464]{3,2,1,0:T(8,128)(2,1)S(1)}, u32[]{:S(2)}, u32[]{:S(2)}) async-start(bf16[4,4,64,464]{3,2,1,0:T(8,128)(2,1)} %get-tuple-element.18), calls=%async_computation.2 | async-start | bytes 2097152 | tf_op jit(solution)/shard_map/all_to_all | solution.py:134
  84.3 9.2 %psum.21 = f32[1856]{0:T(1024)S(1)} all-reduce(f32[1856]{0:T(1024)S(1)} %get-tuple-element.19), channel_id=1, replica_groups=mesh['y'=4,'zl'=4,'c'=2,'zh'=4,'x'=4] {'zl'}, use_global_device_ids=true, to_apply=%region_1.0 | all-reduce | flops 1856 | bytes 14848 | tf_op jit(solution)/shard_map/psum | solution.py:136
  93.5 3.3 %all-to-all-done.2 = bf16[4,4,64,464]{3,2,1,0:T(8,128)(2,1)S(1)} async-done(((bf16[4,4,64,464]{3,2,1,0:T(8,128)(2,1)}), bf16[4,4,64,464]{3,2,1,0:T(8,128)(2,1)S(1)}, u32[]{:S(2)}, u32[]{:S(2)}) %all-to-all-start.2) | async-done | bytes 950304 | tf_op jit(solution)/shard_map/all_to_all | solution.py:134
  96.7 0.9 reduce_sum.24
  97.6 8.9 %all-to-all-start.3 = ((bf16[4,64,464]{2,1,0:T(8,128)(2,1)}), bf16[4,64,464]{2,1,0:T(8,128)(2,1)S(1)}, u32[]{:S(2)}, u32[]{:S(2)}) async-start(bf16[4,64,464]{2,1,0:T(8,128)(2,1)} %reduce_sum.24), calls=%async_computation.3 | async-start | bytes 524288 | tf_op jit(solution)/shard_map/all_to_all | solution.py:139
  106.5 9.0 %psum.22 = f32[1856]{0:T(1024)S(1)} all-reduce(f32[1856]{0:T(1024)S(1)} %psum.21), channel_id=1, replica_groups=mesh['y'=4,'zl'=4,'c'=2,'zh'=4,'x'=4] {'y'}, use_global_device_ids=true, to_apply=%region_3.0 | all-reduce | flops 1856 | bytes 14848 | tf_op jit(solution)/shard_map/psum | solution.py:141
  115.5 3.1 %psum.23 = f32[1856]{0:T(1024)} all-reduce(f32[1856]{0:T(1024)S(1)} %psum.22), channel_id=1, replica_groups=mesh['y'=4,'zl'=4,'c'=2,'zh'=4,'x'=4] {'c'}, use_global_device_ids=true, to_apply=%region_4.0 | all-reduce | flops 1856 | bytes 14848 | tf_op jit(solution)/shard_map/psum | solution.py:141
  118.6 6.1 %all-to-all-done.3 = bf16[4,64,464]{2,1,0:T(8,128)(2,1)S(1)} async-done(((bf16[4,64,464]{2,1,0:T(8,128)(2,1)}), bf16[4,64,464]{2,1,0:T(8,128)(2,1)S(1)}, u32[]{:S(2)}, u32[]{:S(2)}) %all-to-all-start.3) | async-done | bytes 237600 | tf_op jit(solution)/shard_map/all_to_all | solution.py:139
  124.7 0.7 reduce_sum.25
Async XLA Ops:
  22.5 6.0 %copy-start.1 = (bf16[64,464]{1,0:T(8,128)(2,1)S(1)}, bf16[64,464]{1,0:T(8,128)(2,1)}, u32[]{:S(2)}) copy-start(bf16[64,464]{1,0:T(8,128)(2,1)} %param.6) | copy-start | bytes 178180
  22.5 49.4 %copy-start = (f32[1856]{0:T(1024)S(1)}, f32[1856]{0:T(1024)}, u32[]{:S(2)}) copy-start(f32[1856]{0:T(1024)} %steps.1) | copy-start | bytes 22276
  22.5 32.0 %all-to-all-start.1 = ((bf16[4,4,32,1856]{3,2,1,0:T(8,128)(2,1)}), bf16[4,4,32,1856]{3,2,1,0:T(8,128)(2,1)S(1)}, u32[]{:S(2)}, u32[]{:S(2)}) async-start(bf16[4,4,32,1856]{3,2,1,0:T(8,128)(2,1)} %broadcast_in_dim.5), calls=%async_computation.1 | async-start | bytes 3932160 | tf_op jit(solution)/shard_map/all_to_all | solution.py:116
  54.5 17.4 %collective-permute-start = (bf16[4,4,32,1856]{3,2,1,0:T(8,128)(2,1)S(1)}, bf16[4,4,32,1856]{3,2,1,0:T(8,128)(2,1)S(1)}, u32[]{:S(2)}, u32[]{:S(2)}) collective-permute-start(bf16[4,4,32,1856]{3,2,1,0:T(8,128)(2,1)S(1)} %all-to-all-done.1), channel_id=1, source_target_pairs={{0,16},{16,0},{1,17},{17,1},{2,18},{18,2},{3,19},{19,3},{4,20},{20... | collective-permute-start | bytes 5701640 | tf_op jit(solution)/shard_map/ppermute | solution.py:130
  79.7 17.0 %all-to-all-start.2 = ((bf16[4,4,64,464]{3,2,1,0:T(8,128)(2,1)}), bf16[4,4,64,464]{3,2,1,0:T(8,128)(2,1)S(1)}, u32[]{:S(2)}, u32[]{:S(2)}) async-start(bf16[4,4,64,464]{3,2,1,0:T(8,128)(2,1)} %get-tuple-element.18), calls=%async_computation.2 | async-start | bytes 2097152 | tf_op jit(solution)/shard_map/all_to_all | solution.py:134
  97.6 27.0 %all-to-all-start.3 = ((bf16[4,64,464]{2,1,0:T(8,128)(2,1)}), bf16[4,64,464]{2,1,0:T(8,128)(2,1)S(1)}, u32[]{:S(2)}, u32[]{:S(2)}) async-start(bf16[4,64,464]{2,1,0:T(8,128)(2,1)} %reduce_sum.24), calls=%async_computation.3 | async-start | bytes 524288 | tf_op jit(solution)/shard_map/all_to_all | solution.py:139

commit v6 on v5

--- a/solution.py
+++ b/solution.py
@@ -40,6 +40,10 @@
     features, channels = w.shape
     tiles = [(a, min(a + TILE, channels)) for a in range(0, channels, TILE)]
 
+    for z in range(4):
+        tokens = [act[z, y, pl.ds(at, 32), :] for y in range(4) for at in (at_own, at_other)]
+        rows[:, 256 * z : 256 * z + 256] = jnp.concatenate(tokens, axis=0).T
+
     for (top, bottom), load in zip(HALVES, loads):
         load.wait()
         for a, b in tiles:
@@ -59,10 +63,6 @@
                     sums[z, y, pl.ds(at, 32), top:bottom] = part[32 * (4 * y + z) : 32 * (4 * y + z) + 32]
     stores = [pltpu.make_async_copy(sums, sums_hbm, sems.at[2])]
     stores[0].start()
-
-    for z in range(4):
-        tokens = [act[z, y, pl.ds(at, 32), :] for y in range(4) for at in (at_own, at_other)]
-        rows[:, 256 * z : 256 * z + 256] = jnp.concatenate(tokens, axis=0).T
 
     scale = 1.0 / jnp.sqrt(jnp.full((1, 128), 32 * features * high, jnp.float32))
     for n, (top, bottom) in enumerate(HALVES):
@@ -109,7 +109,7 @@
             bytes_accessed=2 * (2 * features * channels + 1024 * (2 * features + channels)),
             transcendentals=0,
         ),
-    )(bounds, *map(resident, (own, other, act)), distant(weight), steps)
+    )(pltpu.with_memory_space_constraint(bounds, pltpu.SMEM), *map(resident, (own, other, act)), distant(weight), steps)
 
 
 def gather(block, axis):
@@ -119,7 +119,7 @@
 def shards(activations, output_grads, weight, step_sizes, level_low, level_high):
     f32, bf16 = jnp.float32, jnp.bfloat16
 
-    grads = gather(output_grads, "zl")
+    grads = lax.all_gather(output_grads, "zl", axis=0)
     grads, activations = tie((grads, activations))
 
     own = gather(grads, "y")

time: 126 us -> 122 us (0.968)
  waiting for transfers between devices: 9.37 us -> 6.78 us
    all_to_all x1 -> x0, blocking collectives: 19.5 us -> none  [gather(): lax.all_to_all(jnp.broadcast_to(block[None], (4, *block.shape)), axis, 0, 0)]
    all_gather x0 -> x1, blocking collectives: none -> 16.8 us  [shards(): grads = lax.all_gather(output_grads, 'zl', axis=0)]
    psum x1, blocking collectives: 9.18 us -> 10.8 us  [shards(): total = lax.psum(total, 'zl')]
    all_to_all x1, waiting for transfers between devices: 3.25 us -> 1.6 us  [shards(): sums = lax.all_to_all(sums, 'x', 0, 0)]
where the time goes in v6:
time: 122 us
  blocking collectives  83.1 us (68%)
  starting transfers between devices  18.8 us (15%)
  Pallas kernels  7.78 us (6%)
  waiting for transfers between devices  6.78 us (6%)
  between operations  1.98 us (2%)
  other arithmetic  1.68 us (1%)
  local copies, waits for them, and re-layouts  1.46 us (1%)
    all_gather x1, blocking collectives, shards(): act = lax.all_gather(activations, 'zh', axis=0)  26.8 us
    all_gather x1, blocking collectives, shards(): grads = lax.all_gather(output_grads, 'zl', axis=0)  16.8 us
    all_gather x1, blocking collectives, shards(): act = lax.all_gather(act, 'x', axis=0)  15.5 us
    psum x2, blocking collectives, shards(): return (input_grads, weight_grads, lax.psum(lax.psum(total, 'y'), 'c'))  13.1 us
    psum x1, blocking collectives, shards(): total = lax.psum(total, 'zl')  10.8 us
    all_to_all x1, starting transfers between devices, shards(): sums = lax.all_to_all(sums, 'zh', 0, 0)  7.83 us
    pallas_call x1, Pallas kernels, products(): pl.pallas_call(products_kernel, out_shape=(pltpu.HBM((4, 4, 64, features)...  7.78 us
    all_to_all x1, waiting for transfers between devices, shards(): sums = lax.all_to_all(sums, 'zh', 0, 0)  5.17 us
  transfers between devices with their start and end apart: 4, of which 2 were waited for; matrix products, arithmetic and copies ran while one was open for 0% of the time, Pallas kernels for 0%

profile of v6, /device:TPU:2, one launch (start us, length us, event | category | flops | bytes accessed | tf_op | source)
XLA Modules:
  0.0 121.5 jit_solution(12446798993774357464)
XLA Ops:
  0.6 16.8 %all-gather = bf16[128,1856]{1,0:T(8,128)(2,1)S(1)} all-gather(bf16[32,1856]{1,0:T(8,128)(2,1)} %param.7), channel_id=2, replica_groups=mesh['y'=4,'zl'=4,'c'=2,'zh'=4,'x'=4] {'zl'}, dimensions={0}, use_global_device_ids=true | all-gather | bytes 593920 | tf_op jit(solution)/shard_map/all_gather | solution.py:122
  17.4 1.4 %broadcast_in_dim.2 = bf16[4,4,32,1856]{3,2,1,0:T(8,128)(2,1)} broadcast(bf16[4,32,1856]{2,1,0:T(8,128)(2,1)S(1)} %bitcast.8), dimensions={1,2,3} | broadcast | bytes 2375680 | tf_op jit(solution)/shard_map/broadcast_in_dim | solution.py:116
  18.8 0.0 copy-start.1
  18.9 0.0 copy-start
  18.9 4.6 %all-to-all-start = ((bf16[4,4,32,1856]{3,2,1,0:T(8,128)(2,1)}), bf16[4,4,32,1856]{3,2,1,0:T(8,128)(2,1)S(1)}, u32[]{:S(2)}, u32[]{:S(2)}) async-start(bf16[4,4,32,1856]{3,2,1,0:T(8,128)(2,1)} %broadcast_in_dim.2), calls=%async_computation | async-start | bytes 3932160 | tf_op jit(solution)/shard_map/all_to_all | solution.py:116
  24.7 0.0 copy-done.1
  24.8 26.8 %all-gather.1 = bf16[256,464]{1,0:T(8,128)(2,1)S(1)} all-gather(bf16[64,464]{1,0:T(8,128)(2,1)S(1)} %copy-done.1), channel_id=3, replica_groups=mesh['y'=4,'zl'=4,'c'=2,'zh'=4,'x'=4] {'zh'}, dimensions={0}, use_global_device_ids=true | all-gather | bytes 296960 | tf_op jit(solution)/shard_map/all_gather | solution.py:126
  51.6 0.1 add_convert_fusion.bounds
  51.6 0.0 all-to-all-done
  51.6 1.9 %collective-permute-start = (bf16[4,4,32,1856]{3,2,1,0:T(8,128)(2,1)S(1)}, bf16[4,4,32,1856]{3,2,1,0:T(8,128)(2,1)S(1)}, u32[]{:S(2)}, u32[]{:S(2)}) collective-permute-start(bf16[4,4,32,1856]{3,2,1,0:T(8,128)(2,1)S(1)} %all-to-all-done), channel_id=1, source_target_pairs={{0,16},{16,0},{1,17},{17,1},{2,18},{18,2},{3,19},{19,3},{4,20},{20... | collective-permute-start | bytes 5701640 | tf_op jit(solution)/shard_map/ppermute | solution.py:130
  53.6 15.5 %all-gather.2 = bf16[16,64,464]{2,1,0:T(8,128)(2,1)S(1)} all-gather(bf16[4,64,464]{2,1,0:T(8,128)(2,1)S(1)} %bitcast.9), channel_id=4, replica_groups=mesh['y'=4,'zl'=4,'c'=2,'zh'=4,'x'=4] {'x'}, dimensions={0}, use_global_device_ids=true | all-gather | bytes 1187840 | tf_op jit(solution)/shard_map/all_gather | solution.py:131
  69.1 0.0 collective-permute-done
  69.1 0.0 copy-done
  69.1 7.8 %shard_map.85 = (bf16[4,4,64,464]{3,2,1,0:T(8,128)(2,1)}, bf16[464,1856]{1,0:T(8,128)(2,1)}, f32[1856]{0:T(1024)S(1)}) custom-call(f32[2]{0:T(128)S(1)} %add_convert_fusion.bounds, bf16[16,32,1856]{2,1,0:T(8,128)(2,1)S(1)} %bitcast.5, bf16[16,32,1856]{2,1,0:T(8,128)(2,1)S(1)} %bitcast.7, bf16[4,4,64,464]{3,2,1,0:T(8,128)(2,1)S(1)} %bitcast.6, ...), custom_call_target="tpu_custom_call" | custom-call | flops 3527409664 | bytes 9146368 | tf_op jit(solution)/shard_map/pallas_call | solution.py:89
  76.9 4.5 %all-to-all-start.1 = ((bf16[4,4,64,464]{3,2,1,0:T(8,128)(2,1)}), bf16[4,4,64,464]{3,2,1,0:T(8,128)(2,1)S(1)}, u32[]{:S(2)}, u32[]{:S(2)}) async-start(bf16[4,4,64,464]{3,2,1,0:T(8,128)(2,1)} %get-tuple-element.18), calls=%async_computation.1 | async-start | bytes 2097152 | tf_op jit(solution)/shard_map/all_to_all | solution.py:134
  81.3 10.8 %psum.21 = f32[1856]{0:T(1024)S(1)} all-reduce(f32[1856]{0:T(1024)S(1)} %get-tuple-element.19), channel_id=1, replica_groups=mesh['y'=4,'zl'=4,'c'=2,'zh'=4,'x'=4] {'zl'}, use_global_device_ids=true, to_apply=%region_1.0 | all-reduce | flops 1856 | bytes 14848 | tf_op jit(solution)/shard_map/psum | solution.py:136
  92.2 1.6 %all-to-all-done.1 = bf16[4,4,64,464]{3,2,1,0:T(8,128)(2,1)S(1)} async-done(((bf16[4,4,64,464]{3,2,1,0:T(8,128)(2,1)}), bf16[4,4,64,464]{3,2,1,0:T(8,128)(2,1)S(1)}, u32[]{:S(2)}, u32[]{:S(2)}) %all-to-all-start.1) | async-done | bytes 950304 | tf_op jit(solution)/shard_map/all_to_all | solution.py:134
  93.8 0.9 reduce_sum.24
  94.7 7.8 %all-to-all-start.2 = ((bf16[4,64,464]{2,1,0:T(8,128)(2,1)}), bf16[4,64,464]{2,1,0:T(8,128)(2,1)S(1)}, u32[]{:S(2)}, u32[]{:S(2)}) async-start(bf16[4,64,464]{2,1,0:T(8,128)(2,1)} %reduce_sum.24), calls=%async_computation.2 | async-start | bytes 524288 | tf_op jit(solution)/shard_map/all_to_all | solution.py:139
  102.6 10.0 %psum.22 = f32[1856]{0:T(1024)S(1)} all-reduce(f32[1856]{0:T(1024)S(1)} %psum.21), channel_id=1, replica_groups=mesh['y'=4,'zl'=4,'c'=2,'zh'=4,'x'=4] {'y'}, use_global_device_ids=true, to_apply=%region_3.0 | all-reduce | flops 1856 | bytes 14848 | tf_op jit(solution)/shard_map/psum | solution.py:141
  112.6 3.1 %psum.23 = f32[1856]{0:T(1024)} all-reduce(f32[1856]{0:T(1024)S(1)} %psum.22), channel_id=1, replica_groups=mesh['y'=4,'zl'=4,'c'=2,'zh'=4,'x'=4] {'c'}, use_global_device_ids=true, to_apply=%region_4.0 | all-reduce | flops 1856 | bytes 14848 | tf_op jit(solution)/shard_map/psum | solution.py:141
  115.7 5.2 %all-to-all-done.2 = bf16[4,64,464]{2,1,0:T(8,128)(2,1)S(1)} async-done(((bf16[4,64,464]{2,1,0:T(8,128)(2,1)}), bf16[4,64,464]{2,1,0:T(8,128)(2,1)S(1)}, u32[]{:S(2)}, u32[]{:S(2)}) %all-to-all-start.2) | async-done | bytes 237600 | tf_op jit(solution)/shard_map/all_to_all | solution.py:139
  120.9 0.7 reduce_sum.25
Async XLA Ops:
  18.8 5.9 %copy-start.1 = (bf16[64,464]{1,0:T(8,128)(2,1)S(1)}, bf16[64,464]{1,0:T(8,128)(2,1)}, u32[]{:S(2)}) copy-start(bf16[64,464]{1,0:T(8,128)(2,1)} %param.6) | copy-start | bytes 178180
  18.9 50.2 %copy-start = (f32[1856]{0:T(1024)S(1)}, f32[1856]{0:T(1024)}, u32[]{:S(2)}) copy-start(f32[1856]{0:T(1024)} %steps.1) | copy-start | bytes 22276
  18.9 32.8 %all-to-all-start = ((bf16[4,4,32,1856]{3,2,1,0:T(8,128)(2,1)}), bf16[4,4,32,1856]{3,2,1,0:T(8,128)(2,1)S(1)}, u32[]{:S(2)}, u32[]{:S(2)}) async-start(bf16[4,4,32,1856]{3,2,1,0:T(8,128)(2,1)} %broadcast_in_dim.2), calls=%async_computation | async-start | bytes 3932160 | tf_op jit(solution)/shard_map/all_to_all | solution.py:116
  51.6 17.4 %collective-permute-start = (bf16[4,4,32,1856]{3,2,1,0:T(8,128)(2,1)S(1)}, bf16[4,4,32,1856]{3,2,1,0:T(8,128)(2,1)S(1)}, u32[]{:S(2)}, u32[]{:S(2)}) collective-permute-start(bf16[4,4,32,1856]{3,2,1,0:T(8,128)(2,1)S(1)} %all-to-all-done), channel_id=1, source_target_pairs={{0,16},{16,0},{1,17},{17,1},{2,18},{18,2},{3,19},{19,3},{4,20},{20... | collective-permute-start | bytes 5701640 | tf_op jit(solution)/shard_map/ppermute | solution.py:130
  76.9 16.9 %all-to-all-start.1 = ((bf16[4,4,64,464]{3,2,1,0:T(8,128)(2,1)}), bf16[4,4,64,464]{3,2,1,0:T(8,128)(2,1)S(1)}, u32[]{:S(2)}, u32[]{:S(2)}) async-start(bf16[4,4,64,464]{3,2,1,0:T(8,128)(2,1)} %get-tuple-element.18), calls=%async_computation.1 | async-start | bytes 2097152 | tf_op jit(solution)/shard_map/all_to_all | solution.py:134
  94.7 26.1 %all-to-all-start.2 = ((bf16[4,64,464]{2,1,0:T(8,128)(2,1)}), bf16[4,64,464]{2,1,0:T(8,128)(2,1)S(1)}, u32[]{:S(2)}, u32[]{:S(2)}) async-start(bf16[4,64,464]{2,1,0:T(8,128)(2,1)} %reduce_sum.24), calls=%async_computation.2 | async-start | bytes 524288 | tf_op jit(solution)/shard_map/all_to_all | solution.py:139

commit v7 on v6

--- a/solution.py
+++ b/solution.py
@@ -138,7 +138,7 @@
 
     sums = lax.all_to_all(sums, "zh", 0, 0)
     input_grads = jnp.sum(sums.astype(f32), axis=0).astype(bf16)
-    return (input_grads, weight_grads, lax.psum(lax.psum(total, "y"), "c"))
+    return (input_grads, weight_grads, lax.psum(lax.psum(total, "c"), "y"))
 
 
 def solution(mesh):

time: 122 us -> 122 us (level)
  no operation moved by 1% of the time
where the time goes in v7:
time: 122 us
  blocking collectives  83 us (68%)
  starting transfers between devices  18.8 us (15%)
  Pallas kernels  7.78 us (6%)
  waiting for transfers between devices  6.82 us (6%)
  between operations  1.97 us (2%)
  other arithmetic  1.68 us (1%)
  local copies, waits for them, and re-layouts  1.46 us (1%)
    all_gather x1, blocking collectives, shards(): act = lax.all_gather(activations, 'zh', axis=0)  26.8 us
    all_gather x1, blocking collectives, shards(): grads = lax.all_gather(output_grads, 'zl', axis=0)  16.8 us
    all_gather x1, blocking collectives, shards(): act = lax.all_gather(act, 'x', axis=0)  15.5 us
    psum x2, blocking collectives, shards(): return (input_grads, weight_grads, lax.psum(lax.psum(total, 'c'), 'y'))  13.1 us
    psum x1, blocking collectives, shards(): total = lax.psum(total, 'zl')  10.8 us
    all_to_all x1, starting transfers between devices, shards(): sums = lax.all_to_all(sums, 'zh', 0, 0)  7.83 us
    pallas_call x1, Pallas kernels, products(): pl.pallas_call(products_kernel, out_shape=(pltpu.HBM((4, 4, 64, features)...  7.78 us
    all_to_all x1, waiting for transfers between devices, shards(): sums = lax.all_to_all(sums, 'zh', 0, 0)  5.21 us
  transfers between devices with their start and end apart: 4, of which 2 were waited for; matrix products, arithmetic and copies ran while one was open for 0% of the time, Pallas kernels for 0%

profile of v7, /device:TPU:2, one launch (start us, length us, event | category | flops | bytes accessed | tf_op | source)
XLA Modules:
  0.0 121.5 jit_solution(11939109967865513410)
XLA Ops:
  0.6 16.8 %all-gather = bf16[128,1856]{1,0:T(8,128)(2,1)S(1)} all-gather(bf16[32,1856]{1,0:T(8,128)(2,1)} %param.7), channel_id=2, replica_groups=mesh['y'=4,'zl'=4,'c'=2,'zh'=4,'x'=4] {'zl'}, dimensions={0}, use_global_device_ids=true | all-gather | bytes 593920 | tf_op jit(solution)/shard_map/all_gather | solution.py:122
  17.4 1.4 %broadcast_in_dim.2 = bf16[4,4,32,1856]{3,2,1,0:T(8,128)(2,1)} broadcast(bf16[4,32,1856]{2,1,0:T(8,128)(2,1)S(1)} %bitcast.8), dimensions={1,2,3} | broadcast | bytes 2375680 | tf_op jit(solution)/shard_map/broadcast_in_dim | solution.py:116
  18.8 0.0 copy-start.1
  18.9 0.0 copy-start
  18.9 4.6 %all-to-all-start = ((bf16[4,4,32,1856]{3,2,1,0:T(8,128)(2,1)}), bf16[4,4,32,1856]{3,2,1,0:T(8,128)(2,1)S(1)}, u32[]{:S(2)}, u32[]{:S(2)}) async-start(bf16[4,4,32,1856]{3,2,1,0:T(8,128)(2,1)} %broadcast_in_dim.2), calls=%async_computation | async-start | bytes 3932160 | tf_op jit(solution)/shard_map/all_to_all | solution.py:116
  24.7 0.0 copy-done.1
  24.8 26.8 %all-gather.1 = bf16[256,464]{1,0:T(8,128)(2,1)S(1)} all-gather(bf16[64,464]{1,0:T(8,128)(2,1)S(1)} %copy-done.1), channel_id=3, replica_groups=mesh['y'=4,'zl'=4,'c'=2,'zh'=4,'x'=4] {'zh'}, dimensions={0}, use_global_device_ids=true | all-gather | bytes 296960 | tf_op jit(solution)/shard_map/all_gather | solution.py:126
  51.6 0.1 add_convert_fusion.bounds
  51.6 0.0 all-to-all-done
  51.6 1.9 %collective-permute-start = (bf16[4,4,32,1856]{3,2,1,0:T(8,128)(2,1)S(1)}, bf16[4,4,32,1856]{3,2,1,0:T(8,128)(2,1)S(1)}, u32[]{:S(2)}, u32[]{:S(2)}) collective-permute-start(bf16[4,4,32,1856]{3,2,1,0:T(8,128)(2,1)S(1)} %all-to-all-done), channel_id=1, source_target_pairs={{0,16},{16,0},{1,17},{17,1},{2,18},{18,2},{3,19},{19,3},{4,20},{20... | collective-permute-start | bytes 5701640 | tf_op jit(solution)/shard_map/ppermute | solution.py:130
  53.6 15.5 %all-gather.2 = bf16[16,64,464]{2,1,0:T(8,128)(2,1)S(1)} all-gather(bf16[4,64,464]{2,1,0:T(8,128)(2,1)S(1)} %bitcast.9), channel_id=4, replica_groups=mesh['y'=4,'zl'=4,'c'=2,'zh'=4,'x'=4] {'x'}, dimensions={0}, use_global_device_ids=true | all-gather | bytes 1187840 | tf_op jit(solution)/shard_map/all_gather | solution.py:131
  69.1 0.0 collective-permute-done
  69.1 0.0 copy-done
  69.1 7.8 %shard_map.85 = (bf16[4,4,64,464]{3,2,1,0:T(8,128)(2,1)}, bf16[464,1856]{1,0:T(8,128)(2,1)}, f32[1856]{0:T(1024)S(1)}) custom-call(f32[2]{0:T(128)S(1)} %add_convert_fusion.bounds, bf16[16,32,1856]{2,1,0:T(8,128)(2,1)S(1)} %bitcast.5, bf16[16,32,1856]{2,1,0:T(8,128)(2,1)S(1)} %bitcast.7, bf16[4,4,64,464]{3,2,1,0:T(8,128)(2,1)S(1)} %bitcast.6, ...), custom_call_target="tpu_custom_call" | custom-call | flops 3527409664 | bytes 9146368 | tf_op jit(solution)/shard_map/pallas_call | solution.py:89
  76.9 4.5 %all-to-all-start.1 = ((bf16[4,4,64,464]{3,2,1,0:T(8,128)(2,1)}), bf16[4,4,64,464]{3,2,1,0:T(8,128)(2,1)S(1)}, u32[]{:S(2)}, u32[]{:S(2)}) async-start(bf16[4,4,64,464]{3,2,1,0:T(8,128)(2,1)} %get-tuple-element.18), calls=%async_computation.1 | async-start | bytes 2097152 | tf_op jit(solution)/shard_map/all_to_all | solution.py:134
  81.3 10.8 %psum.21 = f32[1856]{0:T(1024)S(1)} all-reduce(f32[1856]{0:T(1024)S(1)} %get-tuple-element.19), channel_id=1, replica_groups=mesh['y'=4,'zl'=4,'c'=2,'zh'=4,'x'=4] {'zl'}, use_global_device_ids=true, to_apply=%region_1.0 | all-reduce | flops 1856 | bytes 14848 | tf_op jit(solution)/shard_map/psum | solution.py:136
  92.2 1.6 %all-to-all-done.1 = bf16[4,4,64,464]{3,2,1,0:T(8,128)(2,1)S(1)} async-done(((bf16[4,4,64,464]{3,2,1,0:T(8,128)(2,1)}), bf16[4,4,64,464]{3,2,1,0:T(8,128)(2,1)S(1)}, u32[]{:S(2)}, u32[]{:S(2)}) %all-to-all-start.1) | async-done | bytes 950304 | tf_op jit(solution)/shard_map/all_to_all | solution.py:134
  93.8 0.9 reduce_sum.24
  94.7 7.8 %all-to-all-start.2 = ((bf16[4,64,464]{2,1,0:T(8,128)(2,1)}), bf16[4,64,464]{2,1,0:T(8,128)(2,1)S(1)}, u32[]{:S(2)}, u32[]{:S(2)}) async-start(bf16[4,64,464]{2,1,0:T(8,128)(2,1)} %reduce_sum.24), calls=%async_computation.2 | async-start | bytes 524288 | tf_op jit(solution)/shard_map/all_to_all | solution.py:139
  102.6 2.5 %psum.22 = f32[1856]{0:T(1024)S(1)} all-reduce(f32[1856]{0:T(1024)S(1)} %psum.21), channel_id=1, replica_groups=mesh['y'=4,'zl'=4,'c'=2,'zh'=4,'x'=4] {'c'}, use_global_device_ids=true, to_apply=%region_3.0 | all-reduce | flops 1856 | bytes 14848 | tf_op jit(solution)/shard_map/psum | solution.py:141
  105.0 10.6 %psum.23 = f32[1856]{0:T(1024)} all-reduce(f32[1856]{0:T(1024)S(1)} %psum.22), channel_id=1, replica_groups=mesh['y'=4,'zl'=4,'c'=2,'zh'=4,'x'=4] {'y'}, use_global_device_ids=true, to_apply=%region_4.0 | all-reduce | flops 1856 | bytes 14848 | tf_op jit(solution)/shard_map/psum | solution.py:141
  115.6 5.2 %all-to-all-done.2 = bf16[4,64,464]{2,1,0:T(8,128)(2,1)S(1)} async-done(((bf16[4,64,464]{2,1,0:T(8,128)(2,1)}), bf16[4,64,464]{2,1,0:T(8,128)(2,1)S(1)}, u32[]{:S(2)}, u32[]{:S(2)}) %all-to-all-start.2) | async-done | bytes 237600 | tf_op jit(solution)/shard_map/all_to_all | solution.py:139
  120.9 0.7 reduce_sum.25
Async XLA Ops:
  18.8 5.9 %copy-start.1 = (bf16[64,464]{1,0:T(8,128)(2,1)S(1)}, bf16[64,464]{1,0:T(8,128)(2,1)}, u32[]{:S(2)}) copy-start(bf16[64,464]{1,0:T(8,128)(2,1)} %param.6) | copy-start | bytes 178180
  18.9 50.2 %copy-start = (f32[1856]{0:T(1024)S(1)}, f32[1856]{0:T(1024)}, u32[]{:S(2)}) copy-start(f32[1856]{0:T(1024)} %steps.1) | copy-start | bytes 22276
  18.9 32.8 %all-to-all-start = ((bf16[4,4,32,1856]{3,2,1,0:T(8,128)(2,1)}), bf16[4,4,32,1856]{3,2,1,0:T(8,128)(2,1)S(1)}, u32[]{:S(2)}, u32[]{:S(2)}) async-start(bf16[4,4,32,1856]{3,2,1,0:T(8,128)(2,1)} %broadcast_in_dim.2), calls=%async_computation | async-start | bytes 3932160 | tf_op jit(solution)/shard_map/all_to_all | solution.py:116
  51.6 17.4 %collective-permute-start = (bf16[4,4,32,1856]{3,2,1,0:T(8,128)(2,1)S(1)}, bf16[4,4,32,1856]{3,2,1,0:T(8,128)(2,1)S(1)}, u32[]{:S(2)}, u32[]{:S(2)}) collective-permute-start(bf16[4,4,32,1856]{3,2,1,0:T(8,128)(2,1)S(1)} %all-to-all-done), channel_id=1, source_target_pairs={{0,16},{16,0},{1,17},{17,1},{2,18},{18,2},{3,19},{19,3},{4,20},{20... | collective-permute-start | bytes 5701640 | tf_op jit(solution)/shard_map/ppermute | solution.py:130
  76.9 16.9 %all-to-all-start.1 = ((bf16[4,4,64,464]{3,2,1,0:T(8,128)(2,1)}), bf16[4,4,64,464]{3,2,1,0:T(8,128)(2,1)S(1)}, u32[]{:S(2)}, u32[]{:S(2)}) async-start(bf16[4,4,64,464]{3,2,1,0:T(8,128)(2,1)} %get-tuple-element.18), calls=%async_computation.1 | async-start | bytes 2097152 | tf_op jit(solution)/shard_map/all_to_all | solution.py:134
  94.7 26.1 %all-to-all-start.2 = ((bf16[4,64,464]{2,1,0:T(8,128)(2,1)}), bf16[4,64,464]{2,1,0:T(8,128)(2,1)S(1)}, u32[]{:S(2)}, u32[]{:S(2)}) async-start(bf16[4,64,464]{2,1,0:T(8,128)(2,1)} %reduce_sum.24), calls=%async_computation.2 | async-start | bytes 524288 | tf_op jit(solution)/shard_map/all_to_all | solution.py:139
